TPU v7x, 32 devices: a whole 2x2x4 slice. The times are simulated.
32 devices in a mesh: row: 2 (over core), col: 16 (over z, y, x).
Axes of the slice: x: 2, y: 2, z: 4, core: 2. Of those that a mesh axis runs over, the one named last changes fastest.
Arguments:
- tokens: bfloat16 [272, 8192], P('row', 'col'), may hold values from -6 to 6
- w_in: bfloat16 [8192, 24576], P(None, 'col'), may hold values from -0.0625 to 0.0625
- short_filter: float32 [3, 24576], P(None, 'col'), may hold values from -3.5 to 3.5
- mr_filter: float32 [512, 128], P('col'), may hold values from -0.5 to 0.5
- skip: float32 [8192], P('col'), may hold values from 0.5 to 1.5
- w_out: bfloat16 [8192, 8192], P(None, 'col'), may hold values from -0.0625 to 0.0625
- grad_out: bfloat16 [272, 8192], P('row', 'col'), may hold values from -0.119628906 to 0.119628906
Outputs:
- block_out: bfloat16 [272, 8192], P('row', 'col')
- filter_grad: float32 [512, 128], P('col')
- skip_grad: float32 [8192], P('col')
All inputs are finite; a program needn't handle non-finite values.
Results may differ from a plain program's by a relative error of at most 0.0085.
Values may be sent and summed in bfloat16 or wider, within the bound.
No kernel may reach another device: no remote copies, remote signals or barrier semaphores. Data moves between devices by JAX's collectives and lax.ppermute only.
A program may use at most 128 MiB of HBM per device.

v0:
```python
import functools

import jax
import jax.numpy as jnp
import numpy as np
from jax import lax
from jax.experimental import pallas as pl
from jax.experimental.pallas import tpu as pltpu
from jax.sharding import PartitionSpec as P

F32 = jnp.float32
BF16 = jnp.bfloat16
VMEM_SPEC = pl.BlockSpec(memory_space=pltpu.VMEM)
SMEM_SPEC = pl.BlockSpec(memory_space=pltpu.SMEM)
HBM_SPEC = pl.BlockSpec(memory_space=pltpu.HBM)
WEIGHT_SLOTS = 4
VMEM_LIMIT = 47 * 2**20
SMALL_LIMIT = 16 * 2**20


def split_axis(size):
    low = 1
    while low * low < size and size % (low * 2) == 0:
        low *= 2
    return size // low, low


def low_masks(low, parity):
    bits = [1 << i for i in range(low.bit_length() - 1)]
    return bits[::-1] if parity else bits


def swap_low(block, high, low, step):
    rows = lax.axis_size("row")
    size = high * low
    route = []
    for r in range(rows):
        mask = low_masks(low, r % 2)[step]
        route += [(r * size + c, r * size + (c ^ mask)) for c in range(size)]
    return lax.ppermute(block, ("row", "col"), route)


def shift_high(block, high, low, k):
    route = [(h * low + l, ((h + k) % high) * low + l) for h in range(high) for l in range(low)]
    return lax.ppermute(block, "col", route)


def flipped_low(low):
    parity = lax.axis_index("row") % 2
    forward, backward = low_masks(low, 0), low_masks(low, 1)
    flips = [0]
    for one, other in zip(forward, backward):
        mask = jnp.where(parity == 0, one, other)
        flips += [flip + mask for flip in flips]
    return flips


def after(values, *others):
    return lax.optimization_barrier((values, others))[0]


class Gather:
    def __init__(self, block, high, low, apart):
        self.high, self.low, self.block = high, low, block
        self.bits = low.bit_length() - 1
        shifts = list(range(1, high))
        self.shifts = shifts
        self.line = [shift_high(block, high, low, k) for k in shifts]
        self.near, self.late = [], []
        if apart:
            items = self.plane([block], self.bits - 1)
            self.near = items[1:]
            items = after(items, self.near)
            self.late = [swap_low(each, high, low, self.bits - 1) for each in items]

    def plane(self, items, steps):
        for step in range(steps):
            items = items + [swap_low(each, self.high, self.low, step) for each in items]
        return items

    def pass_on(self, *others):
        self.line = after(self.line, self.near, others)
        blocks = self.line if self.late else [self.block, *self.line]
        self.far = self.plane([jnp.stack(blocks)], self.bits - 1)

    def finish(self, weights, out_type, name, before_hop=()):
        high, low = self.high, self.low
        me = lax.axis_index("col")
        h, l = me // low, me % low
        flips = flipped_low(low)
        from_high = [(h - k + high) % high for k in self.shifts]
        small = weights.size < 2**23
        limit = VMEM_LIMIT if small else 34 * 2**20

        owners = [h * low + (l ^ flip) for flip in flips]
        own = 1 + len(self.near)
        owners, late_owners = owners[:own], owners[own:]
        owners += [f * low + l for f in from_high]
        pieces = [self.block, *self.near, *self.line]
        total, = accumulate(None, pieces, owners, weights, None, F32, 0, limit, name + "_0")
        hop = after(self.far, total, before_hop)
        last = [swap_low(each, high, low, self.bits - 1) for each in hop]
        self.last = last
        if not self.late:
            late_owners, from_high = [], [h, *from_high]
        owners = late_owners + [f * low + (l ^ flip) for flip in flips[1:] for f in from_high]
        final = len(last) * len(from_high)
        loads = final if small else 0
        pieces = [*self.late, *self.far[1:]]
        total, *ahead = accumulate(
            total, pieces, owners, weights, None, F32, loads, limit, name + "_1"
        )
        ahead = ahead[0] if loads else None
        self.total = total
        owners = owners[len(owners) - final :]
        return accumulate(total, last, owners, weights, ahead, out_type, 0, limit, name + "_2")[0]


def accumulate_kernel(counts, has_total, ready, loads, width, owners, *refs):
    refs = list(refs)
    pieces = [refs.pop(0) for _ in counts]
    total = refs.pop(0) if has_total else None
    here = refs.pop(0) if ready else None
    weights, out = refs[:2]
    refs = refs[2:]
    ahead = refs.pop(0) if loads else None
    sums, held, sems, ahead_sems = refs
    order = [(p, i) for p, count in enumerate(counts) for i in range(count or 1)]
    depth = held.shape[1]

    def rows_of(step):
        return weights.at[pl.ds(pl.multiple_of(owners[step] * depth, depth), depth), :]

    def fetch(step):
        slot = step % WEIGHT_SLOTS
        return pltpu.make_async_copy(rows_of(step), held.at[slot], sems.at[slot])

    def load(at):
        return pltpu.make_async_copy(rows_of(len(order) + at), ahead.at[at], ahead_sems.at[at])

    for step in range(ready, min(ready + WEIGHT_SLOTS, len(order))):
        fetch(step).start()
    for step, (p, i) in enumerate(order):
        if step >= ready:
            fetch(step).wait()
        slot = step % WEIGHT_SLOTS
        rows = pieces[p][i] if counts[p] else pieces[p][...]
        for at in range(0, out.shape[1], width):
            cols = slice(at, at + width)
            part = here[step, :, cols] if step < ready else held[slot, :, cols]
            term = jnp.dot(rows, part, preferred_element_type=F32)
            if step == 0 and total is not None:
                term = term + total[:, cols]
            if step:
                term = term + sums[:, cols]
            if step + 1 == len(order):
                out[:, cols] = term.astype(out.dtype)
            else:
                sums[:, cols] = term
        if step >= ready and step + WEIGHT_SLOTS < len(order):
            fetch(step + WEIGHT_SLOTS).start()
        if step == max(0, len(order) - 1 - WEIGHT_SLOTS):
            for at in range(loads):
                load(at).start()
    for at in range(loads):
        load(at).wait()


def accumulate(total, pieces, owners, weights, here, out_type, loads, limit, name):
    counts = tuple(0 if piece.ndim == 2 else piece.shape[0] for piece in pieces)
    rows, depth = pieces[0].shape[-2:]
    columns = weights.shape[-1]
    width = next(w for w in (512, 256, 128, columns) if columns % w == 0)
    steps = sum(count or 1 for count in counts)
    ready = 0 if here is None else here.shape[0]
    operands = [jnp.stack(owners).astype(jnp.int32), *pieces]
    operands += [extra for extra in (total, here) if extra is not None]
    out_shape = [jax.ShapeDtypeStruct((rows, columns), out_type)]
    if loads:
        out_shape.append(jax.ShapeDtypeStruct((loads, depth, columns), weights.dtype))
    return pl.pallas_call(
        functools.partial(accumulate_kernel, counts, total is not None, ready, loads, width),
        out_shape=out_shape,
        in_specs=[SMEM_SPEC] + [VMEM_SPEC] * (len(operands) - 1) + [HBM_SPEC],
        out_specs=[VMEM_SPEC] * len(out_shape),
        scratch_shapes=[
            pltpu.VMEM((rows, columns), F32),
            pltpu.VMEM((WEIGHT_SLOTS, depth, columns), weights.dtype),
            pltpu.SemaphoreType.DMA((WEIGHT_SLOTS,)),
            pltpu.SemaphoreType.DMA((max(1, loads),)),
        ],
        compiler_params=pltpu.CompilerParams(vmem_limit_bytes=limit),
        cost_estimate=pl.CostEstimate(
            flops=2 * steps * rows * depth * columns,
            bytes_accessed=(steps + loads) * depth * columns * 2 + rows * columns * 8,
            transcendentals=0,
        ),
        name=name,
    )(*operands, weights)


def partials_kernel(owners, grads, weights, *refs):
    outs, (held, sems) = refs[:-2], refs[-2:]
    order = [(o, i) for o, out in enumerate(outs) for i in range(out.shape[0])]
    depth = held.shape[1]

    def fetch(step):
        start = pl.multiple_of(owners[step] * depth, depth)
        slot = step % WEIGHT_SLOTS
        return pltpu.make_async_copy(
            weights.at[pl.ds(start, depth), :], held.at[slot], sems.at[slot]
        )

    for step in range(min(WEIGHT_SLOTS, len(order))):
        fetch(step).start()
    for step, (o, i) in enumerate(order):
        fetch(step).wait()
        term = lax.dot_general(
            grads[...],
            held[step % WEIGHT_SLOTS],
            (((1,), (1,)), ((), ())),
            preferred_element_type=F32,
        )
        outs[o][i] = term.astype(outs[o].dtype)
        if step + WEIGHT_SLOTS < len(order):
            fetch(step + WEIGHT_SLOTS).start()


def partials(grads, weights, high, low):
    me = lax.axis_index("col")
    h, l = me // low, me % low
    owners = [((h + j) % high) * low + (l ^ flip) for flip in flipped_low(low) for j in range(high)]
    rows, features = grads.shape
    depth = weights.shape[0] // (high * low)
    counts = [high] + [high << step for step in range(low.bit_length() - 1)]
    return pl.pallas_call(
        partials_kernel,
        out_shape=[jax.ShapeDtypeStruct((count, rows, depth), BF16) for count in counts],
        in_specs=[SMEM_SPEC, VMEM_SPEC, HBM_SPEC],
        out_specs=[VMEM_SPEC] * len(counts),
        scratch_shapes=[
            pltpu.VMEM((WEIGHT_SLOTS, depth, features), weights.dtype),
            pltpu.SemaphoreType.DMA((WEIGHT_SLOTS,)),
        ],
        compiler_params=pltpu.CompilerParams(vmem_limit_bytes=VMEM_LIMIT),
        cost_estimate=pl.CostEstimate(
            flops=2 * rows * features * weights.shape[0],
            bytes_accessed=2 * weights.shape[0] * (features + rows),
            transcendentals=0,
        ),
        name="grad_partials",
    )(jnp.stack(owners).astype(jnp.int32), grads, weights)


def halves(value):
    top = value.astype(BF16)
    return top, (value - top.astype(F32)).astype(BF16)


def prepare_kernel(mr_filter, short_filter, order, table, filters):
    taps, span = table.shape[1:]
    ends = lax.broadcasted_iota(jnp.int32, (taps, span), 0) + lax.broadcasted_iota(
        jnp.int32, (taps, span), 1
    )
    flip = jnp.where(ends == taps, 1.0, 0.0).astype(BF16)
    first = jnp.dot(mr_filter[...].astype(BF16), flip, preferred_element_type=F32)
    for g in range(table.shape[0]):
        spreadout = jnp.broadcast_to(first[g : g + 1, :], (taps, span))
        table[g] = pltpu.roll(spreadout, 0, 1, stride=1, stride_axis=0).astype(table.dtype)
    size = order.shape[0]
    for at in range(0, filters.shape[1], size):
        left = short_filter[:, at : at + size]
        moved = jnp.zeros(left.shape, F32)
        for _ in range(3):
            part = left.astype(BF16)
            moved = moved + jnp.dot(part, order[...], preferred_element_type=F32)
            left = left - part.astype(F32)
        filters[:, at : at + size] = moved


def prepare(mr_filter, short_filter, order):
    groups, taps = mr_filter.shape
    return pl.pallas_call(
        prepare_kernel,
        out_shape=[
            jax.ShapeDtypeStruct((groups, taps, 2 * taps), BF16),
            jax.ShapeDtypeStruct(short_filter.shape, F32),
        ],
        in_specs=[VMEM_SPEC] * 3,
        out_specs=[VMEM_SPEC] * 2,
        compiler_params=pltpu.CompilerParams(vmem_limit_bytes=SMALL_LIMIT),
        name="prepare",
    )(mr_filter, short_filter, order)


def mixing_kernel(groups, earlier, projected, order, filters, bands, skip, gated, query, mixed):
    rows = projected.shape[0]
    channels = skip.shape[1]
    taps = bands.shape[1]
    span = 2 * taps
    extended = jnp.concatenate([earlier[...].astype(F32), projected[...].astype(F32)], 0).astype(BF16)
    lines = jnp.dot(extended, order[...], preferred_element_type=F32)
    short = (
        filters[0:1, :] * lines
        + filters[1:2, :] * pltpu.roll(lines, 1, 0)
        + filters[2:3, :] * pltpu.roll(lines, 2, 0)
    )
    own_query = short[rows:, :channels]
    both = short[:, channels : 2 * channels] * short[:, 2 * channels :]
    query[...] = own_query
    mixed[...] = both
    both_top, both_rest = halves(both)
    pair = jnp.concatenate([both_top, both_rest], 1)
    lane_group = lax.broadcasted_iota(jnp.int32, (taps, channels), 1) // (channels // groups)
    first = spare = rows - taps
    whole = bands[...].reshape(groups * taps, span)
    ends = bands[:, taps - spare :, :].reshape(groups * spare, span)
    bodies = jnp.dot(whole, pair[first : first + span], preferred_element_type=F32)
    tails = jnp.dot(ends, pair[2 * first :], preferred_element_type=F32)
    bodies = bodies[:, :channels] + bodies[:, channels:]
    tails = tails[:, :channels] + tails[:, channels:]
    body, tail = bodies[:taps], tails[:spare]
    for g in range(1, groups):
        body = jnp.where(lane_group == g, bodies[g * taps : (g + 1) * taps], body)
        tail = jnp.where(lane_group[:spare] == g, tails[g * spare : (g + 1) * spare], tail)
    longconv = jnp.concatenate([body, tail], 0)
    gated[...] = (own_query * (longconv + skip[...] * both[rows:])).astype(gated.dtype)


def mixing(earlier, projected, order, filters, bands, skip, groups):
    rows, columns = projected.shape
    channels = columns // 3
    block = order.shape[0] // 3
    steps = channels // block
    per_step = groups // steps
    taps = bands.shape[1]
    ext = 2 * rows
    table = pl.BlockSpec((per_step, taps, 2 * taps), lambda i: (i, 0, 0))
    return pl.pallas_call(
        functools.partial(mixing_kernel, per_step),
        grid=(steps,),
        out_shape=[
            jax.ShapeDtypeStruct((rows, channels), BF16),
            jax.ShapeDtypeStruct((rows, channels), F32),
            jax.ShapeDtypeStruct((ext, channels), F32),
        ],
        in_specs=[
            pl.BlockSpec((rows, 3 * block), lambda i: (0, i)),
            pl.BlockSpec((rows, 3 * block), lambda i: (0, i)),
            pl.BlockSpec((3 * block, 3 * block), lambda i: (0, 0)),
            pl.BlockSpec((3, 3 * block), lambda i: (0, i)),
            table,
            pl.BlockSpec((1, block), lambda i: (0, i)),
        ],
        out_specs=[
            pl.BlockSpec((rows, block), lambda i: (0, i)),
            pl.BlockSpec((rows, block), lambda i: (0, i)),
            pl.BlockSpec((ext, block), lambda i: (0, i)),
        ],
        compiler_params=pltpu.CompilerParams(vmem_limit_bytes=SMALL_LIMIT),
        cost_estimate=pl.CostEstimate(
            flops=2 * 2 * groups * rows * 2 * taps * 2 * block,
            bytes_accessed=4 * ext * channels + 6 * ext * channels + 4 * groups * taps * taps,
            transcendentals=0,
        ),
        name="mixing",
    )(earlier, projected, order, filters, bands, skip)


def tap_grad_kernel(groups, pieces, *refs):
    grads, (query, mixed, taps_out, skip_out) = refs[:pieces], refs[pieces:]
    total = grads[0][...].astype(F32)
    for piece in grads[1:]:
        total = total + piece[...].astype(F32)
    weighted = total * query[...]
    rows, channels = weighted.shape
    taps = taps_out.shape[1]
    span = 2 * taps
    first = rows - taps
    spare = rows - taps
    both = mixed[...]
    skip_out[...] = jnp.sum(weighted * both[rows:], axis=0, keepdims=True)
    both_top = both.astype(BF16)
    flip = jnp.where(
        lax.broadcasted_iota(jnp.int32, (span, span), 0)
        + lax.broadcasted_iota(jnp.int32, (span, span), 1)
        == span - 1,
        1.0,
        0.0,
    ).astype(BF16)

    def backwards(start):
        end = jnp.dot(flip, both_top[start : start + span], preferred_element_type=F32)
        return jnp.concatenate([end.astype(BF16)] * 2, 1)

    near, far = backwards(first), backwards(2 * first)
    parts = jnp.concatenate(halves(weighted), 1)
    lane_group = (lax.broadcasted_iota(jnp.int32, (1, 2 * channels), 1) % channels) // (
        channels // groups
    )
    contract = (((1,), (1,)), ((), ()))
    masks = [jnp.where(lane_group == g, 1.0, 0.0).astype(BF16) for g in range(groups)]
    sides = jnp.concatenate([parts[:taps] * mask for mask in masks], 0)
    ends = jnp.concatenate([parts[taps:].astype(F32) * mask.astype(F32) for mask in masks], 0)
    bodies = lax.dot_general(sides, near, contract, preferred_element_type=F32)
    tails = lax.dot_general(ends.astype(BF16), far, contract, preferred_element_type=F32)
    for g in range(groups):
        body = bodies[g * taps : (g + 1) * taps]
        tail = tails[g * spare : (g + 1) * spare]
        body = jnp.concatenate([body[: taps - spare], body[taps - spare :] + tail], 0)
        skewed = pltpu.roll(body, 0, 1, stride=1, stride_axis=0)
        line = jnp.sum(skewed, axis=0, keepdims=True)
        taps_out[g : g + 1, :] = pltpu.roll(line, span - (taps - 1), 1)[:, :taps]


def tap_grad(grads, query, mixed, groups, taps):
    rows, channels = query.shape
    ext = mixed.shape[0]
    block = 128 if channels % 128 == 0 else channels
    steps = channels // block
    per_step = groups // steps
    span = 2 * taps
    one = pl.BlockSpec((rows, block), lambda i: (0, i))
    return pl.pallas_call(
        functools.partial(tap_grad_kernel, per_step, len(grads)),
        grid=(steps,),
        out_shape=[
            jax.ShapeDtypeStruct((groups, taps), F32),
            jax.ShapeDtypeStruct((1, channels), F32),
        ],
        in_specs=[one] * (len(grads) + 1) + [pl.BlockSpec((ext, block), lambda i: (0, i))],
        out_specs=[
            pl.BlockSpec((per_step, taps), lambda i: (i, 0)),
            pl.BlockSpec((1, block), lambda i: (0, i)),
        ],
        compiler_params=pltpu.CompilerParams(vmem_limit_bytes=SMALL_LIMIT),
        cost_estimate=pl.CostEstimate(
            flops=2 * groups * rows * span * 2 * block,
            bytes_accessed=4 * ext * channels + 6 * rows * channels,
            transcendentals=0,
        ),
        name="tap_grad",
    )(*grads, query, mixed)


def add_pairs_kernel(*refs):
    count = len(refs) // 3
    for one, other, out in zip(refs[:count], refs[count : 2 * count], refs[2 * count :]):
        out[...] = one[...] + other[...]


def add_pairs(ones, others):
    return pl.pallas_call(
        add_pairs_kernel,
        out_shape=[jax.ShapeDtypeStruct(one.shape, one.dtype) for one in ones],
        in_specs=[VMEM_SPEC] * (2 * len(ones)),
        out_specs=[VMEM_SPEC] * len(ones),
        compiler_params=pltpu.CompilerParams(vmem_limit_bytes=SMALL_LIMIT),
        name="add_pairs",
    )(*ones, *others)


def branch_order(block, width):
    to = np.arange(3 * block)
    branch, channel = to // block, to % block
    source = 3 * width * (channel // width) + width * branch + channel % width
    return jnp.asarray(np.arange(3 * block)[:, None] == source[None, :], BF16)


def local(tokens, w_in, short_filter, mr_filter, skip, w_out, grad_out):
    high, low = split_axis(lax.axis_size("col"))
    row_size = lax.axis_size("row")
    channels = tokens.shape[1]
    groups, taps = mr_filter.shape
    width = channels // groups
    block = 128 if channels % 128 == 0 else channels

    order = branch_order(block, width)
    gather = Gather(tokens, high, low, True)
    parts = partials(grad_out, w_out, high, low)
    gather.pass_on(parts, gather.late)
    bands, filters = prepare(*after((mr_filter, short_filter), gather.line), order)
    gather.line = after(gather.line, bands, filters)
    projected = gather.finish(w_in, BF16, "project")
    earlier = lax.ppermute(projected, "row", [(r, r + 1) for r in range(row_size - 1)])
    gated, query, mixed = mixing(earlier, projected, order, filters, bands, skip[None], groups)
    parts = after(parts, gather.total)
    gather = Gather(gated, high, low, True)

    parts = list(parts)
    for step in reversed(range(low.bit_length() - 1)):
        moved = after(swap_low(parts.pop(), high, low, step), gather.near)
        at = 0
        for i, part in enumerate(parts):
            count = part.shape[0]
            total = part.astype(F32) + moved[at : at + count].astype(F32)
            parts[i], at = total.astype(BF16), at + count
    gather.pass_on(gather.late)
    sums = after([parts[0][j] for j in range(high)], gather.line)
    grads = [sums[0]] + [shift_high(sums[j], high, low, j) for j in range(1, high)]
    block_out = gather.finish(w_out, BF16, "output", ())
    grads = after(grads, block_out)

    tap_part, skip_part = tap_grad(grads, query, mixed, groups, taps)
    if row_size == 2:
        swap = [(0, 1), (1, 0)]
        other = [lax.ppermute(part, "row", swap) for part in (tap_part, skip_part)]
        filter_grad, skip_grad = add_pairs((tap_part, skip_part), other)
        skip_grad = skip_grad.reshape(-1)
    else:
        filter_grad, skip_grad = lax.psum((tap_part, skip_part.reshape(-1)), "row")
    return (block_out, filter_grad, skip_grad)


def solution(mesh):
    in_specs = (
        P("row", "col"),
        P(None, "col"),
        P(None, "col"),
        P("col", None),
        P("col"),
        P(None, "col"),
        P("row", "col"),
    )
    out_specs = (P("row", "col"), P("col", None), P("col"))
    return jax.shard_map(local, mesh=mesh, in_specs=in_specs, out_specs=out_specs, check_vma=False)
```

profile of v0, /device:TPU:9, one launch (start us, length us, event | category | flops | bytes accessed | tf_op | source)
XLA Modules:
  0.0 100.8 jit_solution(3593328496819988030)
XLA Ops:
  0.6 1.3 %collective-permute-start.3 = (bf16[136,512]{1,0:T(8,128)(2,1)}, bf16[136,512]{1,0:T(8,128)(2,1)S(1)}, u32[]{:S(2)}, u32[]{:S(2)}) collective-permute-start(bf16[136,512]{1,0:T(8,128)(2,1)} %refs_0_.1), channel_id=1, source_target_pairs={{0,1},{1,0},{2,3},{3,2},{4,5},{5,4},{6,7},{7,6},{8,9},{9,8},{10,11... | collective-permute-start | bytes 417800 | tf_op jit(solution)/shard_map/ppermute | solution.py:40
  2.1 2.3 %collective-permute-start.1 = (bf16[136,512]{1,0:T(8,128)(2,1)}, bf16[136,512]{1,0:T(8,128)(2,1)S(1)}, u32[]{:S(2)}, u32[]{:S(2)}) collective-permute-start(bf16[136,512]{1,0:T(8,128)(2,1)} %refs_0_.1), channel_id=1, source_target_pairs={{0,8},{1,9},{2,10},{3,11},{4,12},{5,13},{6,14},{7,15},{8,0},{9,1},... | collective-permute-start | bytes 417800 | tf_op jit(solution)/shard_map/ppermute | solution.py:45
  4.4 2.2 %collective-permute-start = (bf16[136,512]{1,0:T(8,128)(2,1)}, bf16[136,512]{1,0:T(8,128)(2,1)S(1)}, u32[]{:S(2)}, u32[]{:S(2)}) collective-permute-start(bf16[136,512]{1,0:T(8,128)(2,1)} %refs_0_.1), channel_id=1, source_target_pairs={{0,4},{1,5},{2,6},{3,7},{4,8},{5,9},{6,10},{7,11},{8,12},{9,13},{1... | collective-permute-start | bytes 417800 | tf_op jit(solution)/shard_map/ppermute | solution.py:45
  9.1 7.7 %grad_partials.1 = (bf16[4,136,512]{2,1,0:T(8,128)(2,1)S(1)}, bf16[4,136,512]{2,1,0:T(8,128)(2,1)S(1)}, bf16[8,136,512]{2,1,0:T(8,128)(2,1)}) custom-call(s32[16]{0:T(128)S(1)} %stack.156.owners, bf16[136,512]{1,0:T(8,128)(2,1)S(1)} %copy-done.1, bf16[8192,512]{1,0:T(8,128)(2,1)} %refs_4_.5), custom_call_target="tpu_custom_call" | custom-call | flops 1140850688 | bytes 10616832 | tf_op jit(solution)/shard_map/grad_partials/pallas_call | solution.py:236
  19.6 1.3 %copy-done.9 = bf16[32,128,256]{2,1,0:T(8,128)(2,1)} copy-done((bf16[32,128,256]{2,1,0:T(8,128)(2,1)}, bf16[32,128,256]{2,1,0:T(8,128)(2,1)S(1)}, u32[]{:S(2)}) %copy-start.9) | copy-done | bytes 2097176
  20.9 4.5 %project_0.1.refs_3_ = f32[136,1536]{1,0:T(8,128)S(1)} custom-call(s32[5]{0:T(128)S(1)} %stack.163.owners, bf16[136,512]{1,0:T(8,128)(2,1)S(1)} %copy-done.2, bf16[136,512]{1,0:T(8,128)(2,1)S(1)} %collective-permute-done.3.refs_1_, bf16[136,512]{1,0:T(8,128)(2,1)S(1)} %collective-permute-done.refs_2_, bf16[136,512]{1,0:T(8,128)(2,1)S(1)} %collective-permute-done.1.refs_3_, ...), custom_call_target="tpu_custom_call" | custom-call | flops 1069547520 | bytes 9535488 | tf_op jit(solution)/shard_map/project_0/pallas_call | solution.py:181
  28.2 4.5 %project_1.1.refs_2_ = f32[136,1536]{1,0:T(8,128)S(1)} custom-call(s32[11]{0:T(128)S(1)} %stack.166.owners, bf16[136,512]{1,0:T(8,128)(2,1)S(1)} %copy-done.4, bf16[136,512]{1,0:T(8,128)(2,1)S(1)} %copy-done.6, bf16[3,136,512]{2,1,0:T(8,128)(2,1)S(1)} %collective-permute-done.6.refs_2_, f32[136,1536]{1,0:T(8,128)S(1)} %project_0.1.refs_3_, ...), custom_call_target="tpu_custom_call" | custom-call | flops 1069547520 | bytes 9535488 | tf_op jit(solution)/shard_map/project_1/pallas_call | solution.py:181
  33.9 3.7 %collective-permute-done.8.refs_1_ = bf16[3,136,512]{2,1,0:T(8,128)(2,1)S(1)} collective-permute-done((bf16[3,136,512]{2,1,0:T(8,128)(2,1)S(1)}, bf16[3,136,512]{2,1,0:T(8,128)(2,1)S(1)}, u32[]{:S(2)}, u32[]{:S(2)}) %collective-permute-start.8) | collective-permute-done | bytes 417824 | tf_op jit(solution)/shard_map/ppermute | solution.py:40
  37.7 4.9 %project_2.1.projected = bf16[136,1536]{1,0:T(8,128)(2,1)S(1)} custom-call(s32[6]{0:T(128)S(1)} %stack.70.owners, bf16[3,136,512]{2,1,0:T(8,128)(2,1)S(1)} %collective-permute-done.7.refs_0_, bf16[3,136,512]{2,1,0:T(8,128)(2,1)S(1)} %collective-permute-done.8.refs_1_, f32[136,1536]{1,0:T(8,128)S(1)} %project_1.1.refs_2_, bf16[8192,1536]{1,0:T(8,128)(2,1)} %refs_3_.1), custom_call_target="tpu_custom_call" | custom-call | flops 1283457024 | bytes 11108352 | tf_op jit(solution)/shard_map/project_2/pallas_call | solution.py:181
  43.9 5.1 %collective-permute-done.9.earlier = bf16[136,1536]{1,0:T(8,128)(2,1)S(1)} collective-permute-done((bf16[136,1536]{1,0:T(8,128)(2,1)S(1)}, bf16[136,1536]{1,0:T(8,128)(2,1)S(1)}, u32[]{:S(2)}, u32[]{:S(2)}) %collective-permute-start.9) | collective-permute-done | bytes 417824 | tf_op jit(solution)/shard_map/ppermute | solution.py:485
  49.0 3.0 %mixing.1 = (bf16[136,512]{1,0:T(8,128)(2,1)S(1)}, f32[136,512]{1,0:T(8,128)S(1)}, f32[272,512]{1,0:T(8,128)S(1)}) custom-call(bf16[136,1536]{1,0:T(8,128)(2,1)S(1)} %collective-permute-done.9.earlier, bf16[136,1536]{1,0:T(8,128)(2,1)S(1)} %project_2.1.projected, bf16[384,384]{1,0:T(8,128)(2,1)S(1)} %copy-done, f32[3,1536]{1,0:T(4,128)S(1)} %get-tuple-element.60.filters, ...), custom_call_target="tpu_custom_call" | custom-call | flops 1140850688 | bytes 3489792 | tf_op jit(solution)/shard_map/mixing/pallas_call | solution.py:339
  52.0 1.5 %collective-permute-start.13 = (bf16[136,512]{1,0:T(8,128)(2,1)S(1)}, bf16[136,512]{1,0:T(8,128)(2,1)S(1)}, u32[]{:S(2)}, u32[]{:S(2)}) collective-permute-start(bf16[136,512]{1,0:T(8,128)(2,1)S(1)} %get-tuple-element.67.refs_0_), channel_id=1, source_target_pairs={{0,1},{1,0},{2,3},{3,2},{4,5},{5,4},{6,7},{7,6},{8,9},{9,8},{10,11... | collective-permute-start | bytes 417800 | tf_op jit(solution)/shard_map/ppermute | solution.py:40
  54.3 2.1 %collective-permute-start.10 = (bf16[136,512]{1,0:T(8,128)(2,1)S(1)}, bf16[136,512]{1,0:T(8,128)(2,1)S(1)}, u32[]{:S(2)}, u32[]{:S(2)}) collective-permute-start(bf16[136,512]{1,0:T(8,128)(2,1)S(1)} %get-tuple-element.67.refs_0_), channel_id=1, source_target_pairs={{0,4},{1,5},{2,6},{3,7},{4,8},{5,9},{6,10},{7,11},{8,12},{9,13},{1... | collective-permute-start | bytes 417800 | tf_op jit(solution)/shard_map/ppermute | solution.py:45
  59.1 6.1 %collective-permute-done.12.refs_4_ = bf16[136,512]{1,0:T(8,128)(2,1)S(1)} collective-permute-done((bf16[136,512]{1,0:T(8,128)(2,1)S(1)}, bf16[136,512]{1,0:T(8,128)(2,1)S(1)}, u32[]{:S(2)}, u32[]{:S(2)}) %collective-permute-start.12) | collective-permute-done | bytes 139296 | tf_op jit(solution)/shard_map/ppermute | solution.py:45
  66.1 1.6 %collective-permute-start.16 = (bf16[3,136,512]{2,1,0:T(8,128)(2,1)S(1)}, bf16[3,136,512]{2,1,0:T(8,128)(2,1)S(1)}, u32[]{:S(2)}, u32[]{:S(2)}) collective-permute-start(bf16[3,136,512]{2,1,0:T(8,128)(2,1)S(1)} %pad_maximum_fusion.1), channel_id=1, source_target_pairs={{0,1},{1,0},{2,3},{3,2},{4,5},{5,4},{6,7},{7,6},{8,9},{9,8},{10,11... | collective-permute-start | bytes 1253384 | tf_op jit(solution)/shard_map/ppermute | solution.py:40
  67.6 3.1 %output_0.1.refs_3_ = f32[136,512]{1,0:T(8,128)S(1)} custom-call(s32[5]{0:T(128)S(1)} %stack.163.owners, bf16[136,512]{1,0:T(8,128)(2,1)S(1)} %get-tuple-element.67.refs_0_, bf16[136,512]{1,0:T(8,128)(2,1)S(1)} %collective-permute-done.13.refs_1_, bf16[136,512]{1,0:T(8,128)(2,1)S(1)} %collective-permute-done.10.refs_2_, ...), custom_call_target="tpu_custom_call" | custom-call | flops 356515840 | bytes 3178496 | tf_op jit(solution)/shard_map/output_0/pallas_call | solution.py:181
  70.7 7.6 %collective-permute-done.16.refs_2_ = bf16[3,136,512]{2,1,0:T(8,128)(2,1)S(1)} collective-permute-done((bf16[3,136,512]{2,1,0:T(8,128)(2,1)S(1)}, bf16[3,136,512]{2,1,0:T(8,128)(2,1)S(1)}, u32[]{:S(2)}, u32[]{:S(2)}) %collective-permute-start.16) | collective-permute-done | bytes 417824 | tf_op jit(solution)/shard_map/ppermute | solution.py:40
  78.3 1.5 %collective-permute-start.18 = (bf16[3,136,512]{2,1,0:T(8,128)(2,1)S(1)}, bf16[3,136,512]{2,1,0:T(8,128)(2,1)S(1)}, u32[]{:S(2)}, u32[]{:S(2)}) collective-permute-start(bf16[3,136,512]{2,1,0:T(8,128)(2,1)S(1)} %collective-permute-done.16.refs_2_), channel_id=1, source_target_pairs={{0,2},{1,3},{2,0},{3,1},{4,6},{5,7},{6,4},{7,5},{8,10},{9,11},{10,... | collective-permute-start | bytes 1253384 | tf_op jit(solution)/shard_map/ppermute | solution.py:40
  81.2 1.4 %collective-permute-start.23 = (bf16[136,512]{1,0:T(8,128)(2,1)S(1)}, bf16[136,512]{1,0:T(8,128)(2,1)S(1)}, u32[]{:S(2)}, u32[]{:S(2)}) collective-permute-start(bf16[136,512]{1,0:T(8,128)(2,1)S(1)} %get-tuple-element.84), channel_id=1, source_target_pairs={{0,12},{1,13},{2,14},{3,15},{4,0},{5,1},{6,2},{7,3},{8,4},{9,5},{1... | collective-permute-start | bytes 417800 | tf_op jit(solution)/shard_map/ppermute | solution.py:45
  82.6 3.9 %output_1.1 = (f32[136,512]{1,0:T(8,128)S(1)}, bf16[6,512,512]{2,1,0:T(8,128)(2,1)S(1)}) custom-call(s32[11]{0:T(128)S(1)} %stack.166.owners, bf16[136,512]{1,0:T(8,128)(2,1)S(1)} %collective-permute-done.14.refs_0_, bf16[136,512]{1,0:T(8,128)(2,1)S(1)} %collective-permute-done.15.refs_1_, bf16[3,136,512]{2,1,0:T(8,128)(2,1)S(1)} %collective-permute-done.16.refs_2_, ...), custom_call_target="tpu_custom_call" | custom-call | flops 356515840 | bytes 6324224 | tf_op jit(solution)/shard_map/output_1/pallas_call | solution.py:181
  86.5 3.5 %collective-permute-done.18.refs_1_ = bf16[3,136,512]{2,1,0:T(8,128)(2,1)S(1)} collective-permute-done((bf16[3,136,512]{2,1,0:T(8,128)(2,1)S(1)}, bf16[3,136,512]{2,1,0:T(8,128)(2,1)S(1)}, u32[]{:S(2)}, u32[]{:S(2)}) %collective-permute-start.18) | collective-permute-done | bytes 417824 | tf_op jit(solution)/shard_map/ppermute | solution.py:40
  90.0 1.9 %output_2.1 = bf16[136,512]{1,0:T(8,128)(2,1)} custom-call(s32[6]{0:T(128)S(1)} %stack.70.owners, bf16[3,136,512]{2,1,0:T(8,128)(2,1)S(1)} %collective-permute-done.17.refs_0_, bf16[3,136,512]{2,1,0:T(8,128)(2,1)S(1)} %collective-permute-done.18.refs_1_, f32[136,512]{1,0:T(8,128)S(1)} %get-tuple-element.74.refs_2_, ...), custom_call_target="tpu_custom_call" | custom-call | flops 427819008 | bytes 3702784 | tf_op jit(solution)/shard_map/output_2/pallas_call | solution.py:181
  91.9 3.2 %collective-permute-done.23.refs_3_ = bf16[136,512]{1,0:T(8,128)(2,1)S(1)} collective-permute-done((bf16[136,512]{1,0:T(8,128)(2,1)S(1)}, bf16[136,512]{1,0:T(8,128)(2,1)S(1)}, u32[]{:S(2)}, u32[]{:S(2)}) %collective-permute-start.23) | collective-permute-done | bytes 139296 | tf_op jit(solution)/shard_map/ppermute | solution.py:45
  95.1 3.4 %tap_grad.1 = (f32[32,128]{1,0:T(8,128)S(1)}, f32[1,512]{1,0:T(1,128)S(1)}) custom-call(bf16[136,512]{1,0:T(8,128)(2,1)S(1)} %get-tuple-element.85.refs_0_, bf16[136,512]{1,0:T(8,128)(2,1)S(1)} %collective-permute-done.21.refs_1_, bf16[136,512]{1,0:T(8,128)(2,1)S(1)} %collective-permute-done.22.refs_2_, ...), custom_call_target="tpu_custom_call" | custom-call | flops 570425344 | bytes 974848 | tf_op jit(solution)/shard_map/tap_grad/pallas_call | solution.py:424
  (72 shorter events, 18.8 us)
Async XLA Ops:
  0.6 6.0 %collective-permute-start.3 = (bf16[136,512]{1,0:T(8,128)(2,1)}, bf16[136,512]{1,0:T(8,128)(2,1)S(1)}, u32[]{:S(2)}, u32[]{:S(2)}) collective-permute-start(bf16[136,512]{1,0:T(8,128)(2,1)} %refs_0_.1), channel_id=1, source_target_pairs={{0,1},{1,0},{2,3},{3,2},{4,5},{5,4},{6,7},{7,6},{8,9},{9,8},{10,11... | collective-permute-start | bytes 417800 | tf_op jit(solution)/shard_map/ppermute | solution.py:40
  1.9 14.9 %collective-permute-start.2 = (bf16[136,512]{1,0:T(8,128)(2,1)}, bf16[136,512]{1,0:T(8,128)(2,1)S(1)}, u32[]{:S(2)}, u32[]{:S(2)}) collective-permute-start(bf16[136,512]{1,0:T(8,128)(2,1)} %refs_0_.1), channel_id=1, source_target_pairs={{0,12},{1,13},{2,14},{3,15},{4,0},{5,1},{6,2},{7,3},{8,4},{9,5},{1... | collective-permute-start | bytes 417800 | tf_op jit(solution)/shard_map/ppermute | solution.py:45
  2.1 14.7 %collective-permute-start.1 = (bf16[136,512]{1,0:T(8,128)(2,1)}, bf16[136,512]{1,0:T(8,128)(2,1)S(1)}, u32[]{:S(2)}, u32[]{:S(2)}) collective-permute-start(bf16[136,512]{1,0:T(8,128)(2,1)} %refs_0_.1), channel_id=1, source_target_pairs={{0,8},{1,9},{2,10},{3,11},{4,12},{5,13},{6,14},{7,15},{8,0},{9,1},... | collective-permute-start | bytes 417800 | tf_op jit(solution)/shard_map/ppermute | solution.py:45
  4.4 12.4 %collective-permute-start = (bf16[136,512]{1,0:T(8,128)(2,1)}, bf16[136,512]{1,0:T(8,128)(2,1)S(1)}, u32[]{:S(2)}, u32[]{:S(2)}) collective-permute-start(bf16[136,512]{1,0:T(8,128)(2,1)} %refs_0_.1), channel_id=1, source_target_pairs={{0,4},{1,5},{2,6},{3,7},{4,8},{5,9},{6,10},{7,11},{8,12},{9,13},{1... | collective-permute-start | bytes 417800 | tf_op jit(solution)/shard_map/ppermute | solution.py:45
  6.6 10.3 %collective-permute-start.4 = (bf16[136,512]{1,0:T(8,128)(2,1)}, bf16[136,512]{1,0:T(8,128)(2,1)S(1)}, u32[]{:S(2)}, u32[]{:S(2)}) collective-permute-start(bf16[136,512]{1,0:T(8,128)(2,1)} %refs_0_.1), channel_id=1, source_target_pairs={{0,2},{1,3},{2,0},{3,1},{4,6},{5,7},{6,4},{7,5},{8,10},{9,11},{10,... | collective-permute-start | bytes 417800 | tf_op jit(solution)/shard_map/ppermute | solution.py:40
  7.8 9.1 %collective-permute-start.5 = (bf16[136,512]{1,0:T(8,128)(2,1)S(1)}, bf16[136,512]{1,0:T(8,128)(2,1)S(1)}, u32[]{:S(2)}, u32[]{:S(2)}) collective-permute-start(bf16[136,512]{1,0:T(8,128)(2,1)S(1)} %collective-permute-done.3.refs_1_), channel_id=1, source_target_pairs={{0,2},{1,3},{2,0},{3,1},{4,6},{5,7},{6,4},{7,5},{8,10},{9,11},{10,... | collective-permute-start | bytes 417800 | tf_op jit(solution)/shard_map/ppermute | solution.py:40
  18.4 7.4 %collective-permute-start.6 = (bf16[3,136,512]{2,1,0:T(8,128)(2,1)}, bf16[3,136,512]{2,1,0:T(8,128)(2,1)S(1)}, u32[]{:S(2)}, u32[]{:S(2)}) collective-permute-start(bf16[3,136,512]{2,1,0:T(8,128)(2,1)} %pad_maximum_fusion), channel_id=1, source_target_pairs={{0,1},{1,0},{2,3},{3,2},{4,5},{5,4},{6,7},{7,6},{8,9},{9,8},{10,11... | collective-permute-start | bytes 1253384 | tf_op jit(solution)/shard_map/ppermute | solution.py:40
  25.8 8.1 %collective-permute-start.7 = (bf16[3,136,512]{2,1,0:T(8,128)(2,1)}, bf16[3,136,512]{2,1,0:T(8,128)(2,1)S(1)}, u32[]{:S(2)}, u32[]{:S(2)}) collective-permute-start(bf16[3,136,512]{2,1,0:T(8,128)(2,1)} %pad_maximum_fusion), channel_id=1, source_target_pairs={{0,2},{1,3},{2,0},{3,1},{4,6},{5,7},{6,4},{7,5},{8,10},{9,11},{10,... | collective-permute-start | bytes 1253384 | tf_op jit(solution)/shard_map/ppermute | solution.py:40
  26.9 10.8 %collective-permute-start.8 = (bf16[3,136,512]{2,1,0:T(8,128)(2,1)S(1)}, bf16[3,136,512]{2,1,0:T(8,128)(2,1)S(1)}, u32[]{:S(2)}, u32[]{:S(2)}) collective-permute-start(bf16[3,136,512]{2,1,0:T(8,128)(2,1)S(1)} %collective-permute-done.6.refs_2_), channel_id=1, source_target_pairs={{0,2},{1,3},{2,0},{3,1},{4,6},{5,7},{6,4},{7,5},{8,10},{9,11},{10,... | collective-permute-start | bytes 1253384 | tf_op jit(solution)/shard_map/ppermute | solution.py:40
  32.7 24.8 %collective-permute-start.19 = (bf16[8,136,512]{2,1,0:T(8,128)(2,1)}, bf16[8,136,512]{2,1,0:T(8,128)(2,1)}, u32[]{:S(2)}, u32[]{:S(2)}) collective-permute-start(bf16[8,136,512]{2,1,0:T(8,128)(2,1)} %get-tuple-element.77), channel_id=1, source_target_pairs={{0,2},{1,3},{2,0},{3,1},{4,6},{5,7},{6,4},{7,5},{8,10},{9,11},{10,... | collective-permute-start | bytes 3342344 | tf_op jit(solution)/shard_map/ppermute | solution.py:40
  42.6 6.4 %collective-permute-start.9 = (bf16[136,1536]{1,0:T(8,128)(2,1)S(1)}, bf16[136,1536]{1,0:T(8,128)(2,1)S(1)}, u32[]{:S(2)}, u32[]{:S(2)}) collective-permute-start(bf16[136,1536]{1,0:T(8,128)(2,1)S(1)} %project_2.1.projected), channel_id=1, source_target_pairs={{0,16},{1,17},{2,18},{3,19},{4,20},{5,21},{6,22},{7,23},{8,24},{9,... | collective-permute-start | bytes 1253384 | tf_op jit(solution)/shard_map/ppermute | solution.py:485
  52.0 4.4 %collective-permute-start.13 = (bf16[136,512]{1,0:T(8,128)(2,1)S(1)}, bf16[136,512]{1,0:T(8,128)(2,1)S(1)}, u32[]{:S(2)}, u32[]{:S(2)}) collective-permute-start(bf16[136,512]{1,0:T(8,128)(2,1)S(1)} %get-tuple-element.67.refs_0_), channel_id=1, source_target_pairs={{0,1},{1,0},{2,3},{3,2},{4,5},{5,4},{6,7},{7,6},{8,9},{9,8},{10,11... | collective-permute-start | bytes 417800 | tf_op jit(solution)/shard_map/ppermute | solution.py:40
  53.5 11.7 %collective-permute-start.12 = (bf16[136,512]{1,0:T(8,128)(2,1)S(1)}, bf16[136,512]{1,0:T(8,128)(2,1)S(1)}, u32[]{:S(2)}, u32[]{:S(2)}) collective-permute-start(bf16[136,512]{1,0:T(8,128)(2,1)S(1)} %get-tuple-element.67.refs_0_), channel_id=1, source_target_pairs={{0,12},{1,13},{2,14},{3,15},{4,0},{5,1},{6,2},{7,3},{8,4},{9,5},{1... | collective-permute-start | bytes 417800 | tf_op jit(solution)/shard_map/ppermute | solution.py:45
  53.5 11.7 %collective-permute-start.11 = (bf16[136,512]{1,0:T(8,128)(2,1)S(1)}, bf16[136,512]{1,0:T(8,128)(2,1)S(1)}, u32[]{:S(2)}, u32[]{:S(2)}) collective-permute-start(bf16[136,512]{1,0:T(8,128)(2,1)S(1)} %get-tuple-element.67.refs_0_), channel_id=1, source_target_pairs={{0,8},{1,9},{2,10},{3,11},{4,12},{5,13},{6,14},{7,15},{8,0},{9,1},... | collective-permute-start | bytes 417800 | tf_op jit(solution)/shard_map/ppermute | solution.py:45
  54.3 11.7 %collective-permute-start.10 = (bf16[136,512]{1,0:T(8,128)(2,1)S(1)}, bf16[136,512]{1,0:T(8,128)(2,1)S(1)}, u32[]{:S(2)}, u32[]{:S(2)}) collective-permute-start(bf16[136,512]{1,0:T(8,128)(2,1)S(1)} %get-tuple-element.67.refs_0_), channel_id=1, source_target_pairs={{0,4},{1,5},{2,6},{3,7},{4,8},{5,9},{6,10},{7,11},{8,12},{9,13},{1... | collective-permute-start | bytes 417800 | tf_op jit(solution)/shard_map/ppermute | solution.py:45
  56.4 9.6 %collective-permute-start.14 = (bf16[136,512]{1,0:T(8,128)(2,1)S(1)}, bf16[136,512]{1,0:T(8,128)(2,1)S(1)}, u32[]{:S(2)}, u32[]{:S(2)}) collective-permute-start(bf16[136,512]{1,0:T(8,128)(2,1)S(1)} %get-tuple-element.67.refs_0_), channel_id=1, source_target_pairs={{0,2},{1,3},{2,0},{3,1},{4,6},{5,7},{6,4},{7,5},{8,10},{9,11},{10,... | collective-permute-start | bytes 417800 | tf_op jit(solution)/shard_map/ppermute | solution.py:40
  57.4 8.6 %collective-permute-start.15 = (bf16[136,512]{1,0:T(8,128)(2,1)S(1)}, bf16[136,512]{1,0:T(8,128)(2,1)S(1)}, u32[]{:S(2)}, u32[]{:S(2)}) collective-permute-start(bf16[136,512]{1,0:T(8,128)(2,1)S(1)} %collective-permute-done.13.refs_1_), channel_id=1, source_target_pairs={{0,2},{1,3},{2,0},{3,1},{4,6},{5,7},{6,4},{7,5},{8,10},{9,11},{10,... | collective-permute-start | bytes 417800 | tf_op jit(solution)/shard_map/ppermute | solution.py:40
  65.1 14.6 %collective-permute-start.20 = (bf16[4,136,512]{2,1,0:T(8,128)(2,1)S(1)}, bf16[4,136,512]{2,1,0:T(8,128)(2,1)S(1)}, u32[]{:S(2)}, u32[]{:S(2)}) collective-permute-start(bf16[4,136,512]{2,1,0:T(8,128)(2,1)S(1)} %add_convert_fusion.1), channel_id=1, source_target_pairs={{0,1},{1,0},{2,3},{3,2},{4,5},{5,4},{6,7},{7,6},{8,9},{9,8},{10,11... | collective-permute-start | bytes 1671176 | tf_op jit(solution)/shard_map/ppermute | solution.py:40
  66.1 12.2 %collective-permute-start.16 = (bf16[3,136,512]{2,1,0:T(8,128)(2,1)S(1)}, bf16[3,136,512]{2,1,0:T(8,128)(2,1)S(1)}, u32[]{:S(2)}, u32[]{:S(2)}) collective-permute-start(bf16[3,136,512]{2,1,0:T(8,128)(2,1)S(1)} %pad_maximum_fusion.1), channel_id=1, source_target_pairs={{0,1},{1,0},{2,3},{3,2},{4,5},{5,4},{6,7},{7,6},{8,9},{9,8},{10,11... | collective-permute-start | bytes 1253384 | tf_op jit(solution)/shard_map/ppermute | solution.py:40
  78.3 8.2 %collective-permute-start.17 = (bf16[3,136,512]{2,1,0:T(8,128)(2,1)S(1)}, bf16[3,136,512]{2,1,0:T(8,128)(2,1)S(1)}, u32[]{:S(2)}, u32[]{:S(2)}) collective-permute-start(bf16[3,136,512]{2,1,0:T(8,128)(2,1)S(1)} %pad_maximum_fusion.1), channel_id=1, source_target_pairs={{0,2},{1,3},{2,0},{3,1},{4,6},{5,7},{6,4},{7,5},{8,10},{9,11},{10,... | collective-permute-start | bytes 1253384 | tf_op jit(solution)/shard_map/ppermute | solution.py:40
  78.3 11.7 %collective-permute-start.18 = (bf16[3,136,512]{2,1,0:T(8,128)(2,1)S(1)}, bf16[3,136,512]{2,1,0:T(8,128)(2,1)S(1)}, u32[]{:S(2)}, u32[]{:S(2)}) collective-permute-start(bf16[3,136,512]{2,1,0:T(8,128)(2,1)S(1)} %collective-permute-done.16.refs_2_), channel_id=1, source_target_pairs={{0,2},{1,3},{2,0},{3,1},{4,6},{5,7},{6,4},{7,5},{8,10},{9,11},{10,... | collective-permute-start | bytes 1253384 | tf_op jit(solution)/shard_map/ppermute | solution.py:40
  81.1 10.8 %collective-permute-start.21 = (bf16[136,512]{1,0:T(8,128)(2,1)S(1)}, bf16[136,512]{1,0:T(8,128)(2,1)S(1)}, u32[]{:S(2)}, u32[]{:S(2)}) collective-permute-start(bf16[136,512]{1,0:T(8,128)(2,1)S(1)} %get-tuple-element.82), channel_id=1, source_target_pairs={{0,4},{1,5},{2,6},{3,7},{4,8},{5,9},{6,10},{7,11},{8,12},{9,13},{1... | collective-permute-start | bytes 417800 | tf_op jit(solution)/shard_map/ppermute | solution.py:45
  81.2 10.7 %collective-permute-start.22 = (bf16[136,512]{1,0:T(8,128)(2,1)S(1)}, bf16[136,512]{1,0:T(8,128)(2,1)S(1)}, u32[]{:S(2)}, u32[]{:S(2)}) collective-permute-start(bf16[136,512]{1,0:T(8,128)(2,1)S(1)} %get-tuple-element.83), channel_id=1, source_target_pairs={{0,8},{1,9},{2,10},{3,11},{4,12},{5,13},{6,14},{7,15},{8,0},{9,1},... | collective-permute-start | bytes 417800 | tf_op jit(solution)/shard_map/ppermute | solution.py:45
  81.2 13.8 %collective-permute-start.23 = (bf16[136,512]{1,0:T(8,128)(2,1)S(1)}, bf16[136,512]{1,0:T(8,128)(2,1)S(1)}, u32[]{:S(2)}, u32[]{:S(2)}) collective-permute-start(bf16[136,512]{1,0:T(8,128)(2,1)S(1)} %get-tuple-element.84), channel_id=1, source_target_pairs={{0,12},{1,13},{2,14},{3,15},{4,0},{5,1},{6,2},{7,3},{8,4},{9,5},{1... | collective-permute-start | bytes 417800 | tf_op jit(solution)/shard_map/ppermute | solution.py:45
  (14 other events, 85.1 us)
where the time goes:
time: 101 us
  Pallas kernels  38.2 us (38%)
  waiting for transfers between devices  31.5 us (31%)
  starting transfers between devices  22.7 us (22%)
  local copies, waits for them, and re-layouts  4.25 us (4%)
  other arithmetic  3.32 us (3%)
    pallas_call x6, Pallas kernels, accumulate(): pl.pallas_call(functools.partial(accumulate_kernel, counts, total is not...  22.7 us
    ppermute x14, waiting for transfers between devices, swap_low(): return lax.ppermute(block, ('row', 'col'), route)  15.2 us
    ppermute x14, starting transfers between devices, swap_low(): return lax.ppermute(block, ('row', 'col'), route)  11.6 us
    ppermute x9, waiting for transfers between devices, shift_high(): return lax.ppermute(block, 'col', route)  10.2 us
    ppermute x9, starting transfers between devices, shift_high(): return lax.ppermute(block, 'col', route)  9.1 us
    pallas_call x1, Pallas kernels, partials(): pl.pallas_call(partials_kernel, out_shape=[jax.ShapeDtypeStruct((count, r...  7.73 us
    ppermute x1, waiting for transfers between devices, local(): lax.ppermute(projected, 'row', [(r, r + 1) for r in range(row_size - 1)])  5.14 us
    unnamed x24, local copies, waits for them, and re-layouts  3.86 us
  transfers between devices with their start and end apart: 26, of which 9 were waited for; matrix products, arithmetic and copies ran while one was open for 3% of the time, Pallas kernels for 34%

commit v1 on v0

--- a/solution.py
+++ b/solution.py
@@ -291,6 +291,19 @@
         compiler_params=pltpu.CompilerParams(vmem_limit_bytes=SMALL_LIMIT),
         name="prepare",
     )(mr_filter, short_filter, order)
+
+
+def by_blocks(kernel, steps, parts, *refs):
+    for step in range(steps):
+        views = []
+        for ref, part in zip(refs, parts):
+            if part is not None:
+                size = ref.shape[part] // steps
+                cut = [slice(None)] * len(ref.shape)
+                cut[part] = pl.ds(step * size, size)
+                ref = ref.at[tuple(cut)]
+            views.append(ref)
+        kernel(*views)
 
 
 def mixing_kernel(groups, earlier, projected, order, filters, bands, skip, gated, query, mixed):
@@ -335,29 +348,17 @@
     per_step = groups // steps
     taps = bands.shape[1]
     ext = 2 * rows
-    table = pl.BlockSpec((per_step, taps, 2 * taps), lambda i: (i, 0, 0))
+    parts = (1, 1, None, 1, 0, 1, 1, 1, 1)
     return pl.pallas_call(
-        functools.partial(mixing_kernel, per_step),
-        grid=(steps,),
+        functools.partial(by_blocks, functools.partial(mixing_kernel, per_step), steps, parts),
         out_shape=[
             jax.ShapeDtypeStruct((rows, channels), BF16),
             jax.ShapeDtypeStruct((rows, channels), F32),
             jax.ShapeDtypeStruct((ext, channels), F32),
         ],
-        in_specs=[
-            pl.BlockSpec((rows, 3 * block), lambda i: (0, i)),
-            pl.BlockSpec((rows, 3 * block), lambda i: (0, i)),
-            pl.BlockSpec((3 * block, 3 * block), lambda i: (0, 0)),
-            pl.BlockSpec((3, 3 * block), lambda i: (0, i)),
-            table,
-            pl.BlockSpec((1, block), lambda i: (0, i)),
-        ],
-        out_specs=[
-            pl.BlockSpec((rows, block), lambda i: (0, i)),
-            pl.BlockSpec((rows, block), lambda i: (0, i)),
-            pl.BlockSpec((ext, block), lambda i: (0, i)),
-        ],
-        compiler_params=pltpu.CompilerParams(vmem_limit_bytes=SMALL_LIMIT),
+        in_specs=[VMEM_SPEC] * 6,
+        out_specs=[VMEM_SPEC] * 3,
+        compiler_params=pltpu.CompilerParams(vmem_limit_bytes=2 * SMALL_LIMIT),
         cost_estimate=pl.CostEstimate(
             flops=2 * 2 * groups * rows * 2 * taps * 2 * block,
             bytes_accessed=4 * ext * channels + 6 * ext * channels + 4 * groups * taps * taps,
@@ -420,20 +421,17 @@
     steps = channels // block
     per_step = groups // steps
     span = 2 * taps
-    one = pl.BlockSpec((rows, block), lambda i: (0, i))
+    parts = (1,) * (len(grads) + 2) + (0, 1)
+    kernel = functools.partial(tap_grad_kernel, per_step, len(grads))
     return pl.pallas_call(
-        functools.partial(tap_grad_kernel, per_step, len(grads)),
-        grid=(steps,),
+        functools.partial(by_blocks, kernel, steps, parts),
         out_shape=[
             jax.ShapeDtypeStruct((groups, taps), F32),
             jax.ShapeDtypeStruct((1, channels), F32),
         ],
-        in_specs=[one] * (len(grads) + 1) + [pl.BlockSpec((ext, block), lambda i: (0, i))],
-        out_specs=[
-            pl.BlockSpec((per_step, taps), lambda i: (i, 0)),
-            pl.BlockSpec((1, block), lambda i: (0, i)),
-        ],
-        compiler_params=pltpu.CompilerParams(vmem_limit_bytes=SMALL_LIMIT),
+        in_specs=[VMEM_SPEC] * (len(grads) + 2),
+        out_specs=[VMEM_SPEC] * 2,
+        compiler_params=pltpu.CompilerParams(vmem_limit_bytes=2 * SMALL_LIMIT),
         cost_estimate=pl.CostEstimate(
             flops=2 * groups * rows * span * 2 * block,
             bytes_accessed=4 * ext * channels + 6 * rows * channels,

time: 101 us -> 99.2 us (0.982)
  Pallas kernels: 38.2 us -> 35.8 us
    pallas_call x2, Pallas kernels: 6.37 us -> 4.2 us  [the longest x1 2.29 us: mixing(): pl.pallas_call(functools.partial(by_blocks, functools.partial(mixing_kern...]
where the time goes in v1:
time: 99.2 us; the launch traced here: 98.7 us
  Pallas kernels  35.8 us (36%)
  waiting for transfers between devices  31.3 us (32%)
  starting transfers between devices  23.1 us (23%)
  local copies, waits for them, and re-layouts  4.25 us (4%)
  other arithmetic  3.32 us (3%)
    pallas_call x6, Pallas kernels, accumulate(): pl.pallas_call(functools.partial(accumulate_kernel, counts, total is not...  22.7 us
    ppermute x14, waiting for transfers between devices, swap_low(): return lax.ppermute(block, ('row', 'col'), route)  14.9 us
    ppermute x14, starting transfers between devices, swap_low(): return lax.ppermute(block, ('row', 'col'), route)  12.1 us
    ppermute x9, waiting for transfers between devices, shift_high(): return lax.ppermute(block, 'col', route)  10 us
    ppermute x9, starting transfers between devices, shift_high(): return lax.ppermute(block, 'col', route)  9.04 us
    pallas_call x1, Pallas kernels, partials(): pl.pallas_call(partials_kernel, out_shape=[jax.ShapeDtypeStruct((count, r...  7.6 us
    ppermute x1, waiting for transfers between devices, local(): lax.ppermute(projected, 'row', [(r, r + 1) for r in range(row_size - 1)])  5.4 us
    unnamed x24, local copies, waits for them, and re-layouts  3.86 us
  transfers between devices with their start and end apart: 26, of which 9 were waited for; matrix products, arithmetic and copies ran while one was open for 3% of the time, Pallas kernels for 34%

profile of v1, /device:TPU:9, one launch (start us, length us, event | category | flops | bytes accessed | tf_op | source)
XLA Modules:
  0.0 98.7 jit_solution(4335516873897018022)
XLA Ops:
  2.1 2.3 %collective-permute-start.1 = (bf16[136,512]{1,0:T(8,128)(2,1)}, bf16[136,512]{1,0:T(8,128)(2,1)S(1)}, u32[]{:S(2)}, u32[]{:S(2)}) collective-permute-start(bf16[136,512]{1,0:T(8,128)(2,1)} %refs_0_.1), channel_id=1, source_target_pairs={{0,8},{1,9},{2,10},{3,11},{4,12},{5,13},{6,14},{7,15},{8,0},{9,1},... | collective-permute-start | bytes 417800 | tf_op jit(solution)/shard_map/ppermute | solution.py:45
  4.4 2.2 %collective-permute-start = (bf16[136,512]{1,0:T(8,128)(2,1)}, bf16[136,512]{1,0:T(8,128)(2,1)S(1)}, u32[]{:S(2)}, u32[]{:S(2)}) collective-permute-start(bf16[136,512]{1,0:T(8,128)(2,1)} %refs_0_.1), channel_id=1, source_target_pairs={{0,4},{1,5},{2,6},{3,7},{4,8},{5,9},{6,10},{7,11},{8,12},{9,13},{1... | collective-permute-start | bytes 417800 | tf_op jit(solution)/shard_map/ppermute | solution.py:45
  9.1 7.6 %grad_partials.1 = (bf16[4,136,512]{2,1,0:T(8,128)(2,1)S(1)}, bf16[4,136,512]{2,1,0:T(8,128)(2,1)S(1)}, bf16[8,136,512]{2,1,0:T(8,128)(2,1)}) custom-call(s32[16]{0:T(128)S(1)} %stack.156.owners, bf16[136,512]{1,0:T(8,128)(2,1)S(1)} %copy-done.1, bf16[8192,512]{1,0:T(8,128)(2,1)} %refs_4_.5), custom_call_target="tpu_custom_call" | custom-call | flops 1140850688 | bytes 10616832 | tf_op jit(solution)/shard_map/grad_partials/pallas_call | solution.py:236
  20.9 4.5 %project_0.1.refs_3_ = f32[136,1536]{1,0:T(8,128)S(1)} custom-call(s32[5]{0:T(128)S(1)} %stack.163.owners, bf16[136,512]{1,0:T(8,128)(2,1)S(1)} %copy-done.2, bf16[136,512]{1,0:T(8,128)(2,1)S(1)} %collective-permute-done.3.refs_1_, bf16[136,512]{1,0:T(8,128)(2,1)S(1)} %collective-permute-done.refs_2_, bf16[136,512]{1,0:T(8,128)(2,1)S(1)} %collective-permute-done.1.refs_3_, ...), custom_call_target="tpu_custom_call" | custom-call | flops 1069547520 | bytes 9535488 | tf_op jit(solution)/shard_map/project_0/pallas_call | solution.py:181
  25.7 1.3 %collective-permute-start.7 = (bf16[3,136,512]{2,1,0:T(8,128)(2,1)}, bf16[3,136,512]{2,1,0:T(8,128)(2,1)S(1)}, u32[]{:S(2)}, u32[]{:S(2)}) collective-permute-start(bf16[3,136,512]{2,1,0:T(8,128)(2,1)} %pad_maximum_fusion), channel_id=1, source_target_pairs={{0,2},{1,3},{2,0},{3,1},{4,6},{5,7},{6,4},{7,5},{8,10},{9,11},{10,... | collective-permute-start | bytes 1253384 | tf_op jit(solution)/shard_map/ppermute | solution.py:40
  28.0 4.5 %project_1.1.refs_2_ = f32[136,1536]{1,0:T(8,128)S(1)} custom-call(s32[11]{0:T(128)S(1)} %stack.166.owners, bf16[136,512]{1,0:T(8,128)(2,1)S(1)} %copy-done.4, bf16[136,512]{1,0:T(8,128)(2,1)S(1)} %copy-done.6, bf16[3,136,512]{2,1,0:T(8,128)(2,1)S(1)} %collective-permute-done.6.refs_2_, f32[136,1536]{1,0:T(8,128)S(1)} %project_0.1.refs_3_, ...), custom_call_target="tpu_custom_call" | custom-call | flops 1069547520 | bytes 9535488 | tf_op jit(solution)/shard_map/project_1/pallas_call | solution.py:181
  32.5 1.4 %collective-permute-start.19 = (bf16[8,136,512]{2,1,0:T(8,128)(2,1)}, bf16[8,136,512]{2,1,0:T(8,128)(2,1)}, u32[]{:S(2)}, u32[]{:S(2)}) collective-permute-start(bf16[8,136,512]{2,1,0:T(8,128)(2,1)} %get-tuple-element.77), channel_id=1, source_target_pairs={{0,2},{1,3},{2,0},{3,1},{4,6},{5,7},{6,4},{7,5},{8,10},{9,11},{10,... | collective-permute-start | bytes 3342344 | tf_op jit(solution)/shard_map/ppermute | solution.py:40
  34.1 3.5 %collective-permute-done.8.refs_1_ = bf16[3,136,512]{2,1,0:T(8,128)(2,1)S(1)} collective-permute-done((bf16[3,136,512]{2,1,0:T(8,128)(2,1)S(1)}, bf16[3,136,512]{2,1,0:T(8,128)(2,1)S(1)}, u32[]{:S(2)}, u32[]{:S(2)}) %collective-permute-start.8) | collective-permute-done | bytes 417824 | tf_op jit(solution)/shard_map/ppermute | solution.py:40
  37.5 4.9 %project_2.1.refs_1_ = bf16[136,1536]{1,0:T(8,128)(2,1)S(1)} custom-call(s32[6]{0:T(128)S(1)} %stack.70.owners, bf16[3,136,512]{2,1,0:T(8,128)(2,1)S(1)} %collective-permute-done.7.refs_0_, bf16[3,136,512]{2,1,0:T(8,128)(2,1)S(1)} %collective-permute-done.8.refs_1_, f32[136,1536]{1,0:T(8,128)S(1)} %project_1.1.refs_2_, bf16[8192,1536]{1,0:T(8,128)(2,1)} %refs_3_.1), custom_call_target="tpu_custom_call" | custom-call | flops 1283457024 | bytes 11108352 | tf_op jit(solution)/shard_map/project_2/pallas_call | solution.py:181
  43.7 5.4 %collective-permute-done.9.refs_0_ = bf16[136,1536]{1,0:T(8,128)(2,1)S(1)} collective-permute-done((bf16[136,1536]{1,0:T(8,128)(2,1)S(1)}, bf16[136,1536]{1,0:T(8,128)(2,1)S(1)}, u32[]{:S(2)}, u32[]{:S(2)}) %collective-permute-start.9) | collective-permute-done | bytes 417824 | tf_op jit(solution)/shard_map/ppermute | solution.py:483
  49.2 2.3 %mixing.1 = (bf16[136,512]{1,0:T(8,128)(2,1)S(1)}, f32[136,512]{1,0:T(8,128)S(1)}, f32[272,512]{1,0:T(8,128)S(1)}) custom-call(bf16[136,1536]{1,0:T(8,128)(2,1)S(1)} %collective-permute-done.9.refs_0_, bf16[136,1536]{1,0:T(8,128)(2,1)S(1)} %project_2.1.refs_1_, bf16[384,384]{1,0:T(8,128)(2,1)S(1)} %copy-done, f32[3,1536]{1,0:T(4,128)S(1)} %get-tuple-element.60.refs_3_, ...), custom_call_target="tpu_custom_call" | custom-call | flops 1140850688 | bytes 3489792 | tf_op jit(solution)/shard_map/mixing/pallas_call | solution.py:352
  51.4 1.5 %collective-permute-start.13 = (bf16[136,512]{1,0:T(8,128)(2,1)S(1)}, bf16[136,512]{1,0:T(8,128)(2,1)S(1)}, u32[]{:S(2)}, u32[]{:S(2)}) collective-permute-start(bf16[136,512]{1,0:T(8,128)(2,1)S(1)} %get-tuple-element.67.refs_0_), channel_id=1, source_target_pairs={{0,1},{1,0},{2,3},{3,2},{4,5},{5,4},{6,7},{7,6},{8,9},{9,8},{10,11... | collective-permute-start | bytes 417800 | tf_op jit(solution)/shard_map/ppermute | solution.py:40
  53.7 2.2 %collective-permute-start.10 = (bf16[136,512]{1,0:T(8,128)(2,1)S(1)}, bf16[136,512]{1,0:T(8,128)(2,1)S(1)}, u32[]{:S(2)}, u32[]{:S(2)}) collective-permute-start(bf16[136,512]{1,0:T(8,128)(2,1)S(1)} %get-tuple-element.67.refs_0_), channel_id=1, source_target_pairs={{0,4},{1,5},{2,6},{3,7},{4,8},{5,9},{6,10},{7,11},{8,12},{9,13},{1... | collective-permute-start | bytes 417800 | tf_op jit(solution)/shard_map/ppermute | solution.py:45
  58.5 6.1 %collective-permute-done.12.refs_4_ = bf16[136,512]{1,0:T(8,128)(2,1)S(1)} collective-permute-done((bf16[136,512]{1,0:T(8,128)(2,1)S(1)}, bf16[136,512]{1,0:T(8,128)(2,1)S(1)}, u32[]{:S(2)}, u32[]{:S(2)}) %collective-permute-start.12) | collective-permute-done | bytes 139296 | tf_op jit(solution)/shard_map/ppermute | solution.py:45
  65.3 1.7 %collective-permute-start.16 = (bf16[3,136,512]{2,1,0:T(8,128)(2,1)S(1)}, bf16[3,136,512]{2,1,0:T(8,128)(2,1)S(1)}, u32[]{:S(2)}, u32[]{:S(2)}) collective-permute-start(bf16[3,136,512]{2,1,0:T(8,128)(2,1)S(1)} %pad_maximum_fusion.1), channel_id=1, source_target_pairs={{0,1},{1,0},{2,3},{3,2},{4,5},{5,4},{6,7},{7,6},{8,9},{9,8},{10,11... | collective-permute-start | bytes 1253384 | tf_op jit(solution)/shard_map/ppermute | solution.py:40
  67.0 3.1 %output_0.1.refs_3_ = f32[136,512]{1,0:T(8,128)S(1)} custom-call(s32[5]{0:T(128)S(1)} %stack.163.owners, bf16[136,512]{1,0:T(8,128)(2,1)S(1)} %get-tuple-element.67.refs_0_, bf16[136,512]{1,0:T(8,128)(2,1)S(1)} %collective-permute-done.13.refs_1_, bf16[136,512]{1,0:T(8,128)(2,1)S(1)} %collective-permute-done.10.refs_2_, ...), custom_call_target="tpu_custom_call" | custom-call | flops 356515840 | bytes 3178496 | tf_op jit(solution)/shard_map/output_0/pallas_call | solution.py:181
  70.1 7.7 %collective-permute-done.16.refs_2_ = bf16[3,136,512]{2,1,0:T(8,128)(2,1)S(1)} collective-permute-done((bf16[3,136,512]{2,1,0:T(8,128)(2,1)S(1)}, bf16[3,136,512]{2,1,0:T(8,128)(2,1)S(1)}, u32[]{:S(2)}, u32[]{:S(2)}) %collective-permute-start.16) | collective-permute-done | bytes 417824 | tf_op jit(solution)/shard_map/ppermute | solution.py:40
  77.8 1.5 %collective-permute-start.18 = (bf16[3,136,512]{2,1,0:T(8,128)(2,1)S(1)}, bf16[3,136,512]{2,1,0:T(8,128)(2,1)S(1)}, u32[]{:S(2)}, u32[]{:S(2)}) collective-permute-start(bf16[3,136,512]{2,1,0:T(8,128)(2,1)S(1)} %collective-permute-done.16.refs_2_), channel_id=1, source_target_pairs={{0,2},{1,3},{2,0},{3,1},{4,6},{5,7},{6,4},{7,5},{8,10},{9,11},{10,... | collective-permute-start | bytes 1253384 | tf_op jit(solution)/shard_map/ppermute | solution.py:40
  80.7 1.4 %collective-permute-start.23 = (bf16[136,512]{1,0:T(8,128)(2,1)S(1)}, bf16[136,512]{1,0:T(8,128)(2,1)S(1)}, u32[]{:S(2)}, u32[]{:S(2)}) collective-permute-start(bf16[136,512]{1,0:T(8,128)(2,1)S(1)} %get-tuple-element.84), channel_id=1, source_target_pairs={{0,12},{1,13},{2,14},{3,15},{4,0},{5,1},{6,2},{7,3},{8,4},{9,5},{1... | collective-permute-start | bytes 417800 | tf_op jit(solution)/shard_map/ppermute | solution.py:45
  82.1 3.9 %output_1.1 = (f32[136,512]{1,0:T(8,128)S(1)}, bf16[6,512,512]{2,1,0:T(8,128)(2,1)S(1)}) custom-call(s32[11]{0:T(128)S(1)} %stack.166.owners, bf16[136,512]{1,0:T(8,128)(2,1)S(1)} %collective-permute-done.14.refs_0_, bf16[136,512]{1,0:T(8,128)(2,1)S(1)} %collective-permute-done.15.refs_1_, bf16[3,136,512]{2,1,0:T(8,128)(2,1)S(1)} %collective-permute-done.16.refs_2_, ...), custom_call_target="tpu_custom_call" | custom-call | flops 356515840 | bytes 6324224 | tf_op jit(solution)/shard_map/output_1/pallas_call | solution.py:181
  86.0 3.5 %collective-permute-done.18.refs_1_ = bf16[3,136,512]{2,1,0:T(8,128)(2,1)S(1)} collective-permute-done((bf16[3,136,512]{2,1,0:T(8,128)(2,1)S(1)}, bf16[3,136,512]{2,1,0:T(8,128)(2,1)S(1)}, u32[]{:S(2)}, u32[]{:S(2)}) %collective-permute-start.18) | collective-permute-done | bytes 417824 | tf_op jit(solution)/shard_map/ppermute | solution.py:40
  89.4 1.9 %output_2.1 = bf16[136,512]{1,0:T(8,128)(2,1)} custom-call(s32[6]{0:T(128)S(1)} %stack.70.owners, bf16[3,136,512]{2,1,0:T(8,128)(2,1)S(1)} %collective-permute-done.17.refs_0_, bf16[3,136,512]{2,1,0:T(8,128)(2,1)S(1)} %collective-permute-done.18.refs_1_, f32[136,512]{1,0:T(8,128)S(1)} %get-tuple-element.74.refs_2_, ...), custom_call_target="tpu_custom_call" | custom-call | flops 427819008 | bytes 3702784 | tf_op jit(solution)/shard_map/output_2/pallas_call | solution.py:181
  91.3 3.2 %collective-permute-done.23.refs_3_ = bf16[136,512]{1,0:T(8,128)(2,1)S(1)} collective-permute-done((bf16[136,512]{1,0:T(8,128)(2,1)S(1)}, bf16[136,512]{1,0:T(8,128)(2,1)S(1)}, u32[]{:S(2)}, u32[]{:S(2)}) %collective-permute-start.23) | collective-permute-done | bytes 139296 | tf_op jit(solution)/shard_map/ppermute | solution.py:45
  94.5 1.9 %tap_grad.1 = (f32[32,128]{1,0:T(8,128)S(1)}, f32[1,512]{1,0:T(1,128)S(1)}) custom-call(bf16[136,512]{1,0:T(8,128)(2,1)S(1)} %get-tuple-element.85.refs_0_, bf16[136,512]{1,0:T(8,128)(2,1)S(1)} %collective-permute-done.21.refs_1_, bf16[136,512]{1,0:T(8,128)(2,1)S(1)} %collective-permute-done.22.refs_2_, ...), custom_call_target="tpu_custom_call" | custom-call | flops 570425344 | bytes 974848 | tf_op jit(solution)/shard_map/tap_grad/pallas_call | solution.py:426
  (72 shorter events, 18.5 us)
Async XLA Ops:
  0.6 6.0 %collective-permute-start.3 = (bf16[136,512]{1,0:T(8,128)(2,1)}, bf16[136,512]{1,0:T(8,128)(2,1)S(1)}, u32[]{:S(2)}, u32[]{:S(2)}) collective-permute-start(bf16[136,512]{1,0:T(8,128)(2,1)} %refs_0_.1), channel_id=1, source_target_pairs={{0,1},{1,0},{2,3},{3,2},{4,5},{5,4},{6,7},{7,6},{8,9},{9,8},{10,11... | collective-permute-start | bytes 417800 | tf_op jit(solution)/shard_map/ppermute | solution.py:40
  1.9 14.8 %collective-permute-start.2 = (bf16[136,512]{1,0:T(8,128)(2,1)}, bf16[136,512]{1,0:T(8,128)(2,1)S(1)}, u32[]{:S(2)}, u32[]{:S(2)}) collective-permute-start(bf16[136,512]{1,0:T(8,128)(2,1)} %refs_0_.1), channel_id=1, source_target_pairs={{0,12},{1,13},{2,14},{3,15},{4,0},{5,1},{6,2},{7,3},{8,4},{9,5},{1... | collective-permute-start | bytes 417800 | tf_op jit(solution)/shard_map/ppermute | solution.py:45
  2.1 14.6 %collective-permute-start.1 = (bf16[136,512]{1,0:T(8,128)(2,1)}, bf16[136,512]{1,0:T(8,128)(2,1)S(1)}, u32[]{:S(2)}, u32[]{:S(2)}) collective-permute-start(bf16[136,512]{1,0:T(8,128)(2,1)} %refs_0_.1), channel_id=1, source_target_pairs={{0,8},{1,9},{2,10},{3,11},{4,12},{5,13},{6,14},{7,15},{8,0},{9,1},... | collective-permute-start | bytes 417800 | tf_op jit(solution)/shard_map/ppermute | solution.py:45
  4.4 12.3 %collective-permute-start = (bf16[136,512]{1,0:T(8,128)(2,1)}, bf16[136,512]{1,0:T(8,128)(2,1)S(1)}, u32[]{:S(2)}, u32[]{:S(2)}) collective-permute-start(bf16[136,512]{1,0:T(8,128)(2,1)} %refs_0_.1), channel_id=1, source_target_pairs={{0,4},{1,5},{2,6},{3,7},{4,8},{5,9},{6,10},{7,11},{8,12},{9,13},{1... | collective-permute-start | bytes 417800 | tf_op jit(solution)/shard_map/ppermute | solution.py:45
  6.6 10.1 %collective-permute-start.4 = (bf16[136,512]{1,0:T(8,128)(2,1)}, bf16[136,512]{1,0:T(8,128)(2,1)S(1)}, u32[]{:S(2)}, u32[]{:S(2)}) collective-permute-start(bf16[136,512]{1,0:T(8,128)(2,1)} %refs_0_.1), channel_id=1, source_target_pairs={{0,2},{1,3},{2,0},{3,1},{4,6},{5,7},{6,4},{7,5},{8,10},{9,11},{10,... | collective-permute-start | bytes 417800 | tf_op jit(solution)/shard_map/ppermute | solution.py:40
  7.8 8.9 %collective-permute-start.5 = (bf16[136,512]{1,0:T(8,128)(2,1)S(1)}, bf16[136,512]{1,0:T(8,128)(2,1)S(1)}, u32[]{:S(2)}, u32[]{:S(2)}) collective-permute-start(bf16[136,512]{1,0:T(8,128)(2,1)S(1)} %collective-permute-done.3.refs_1_), channel_id=1, source_target_pairs={{0,2},{1,3},{2,0},{3,1},{4,6},{5,7},{6,4},{7,5},{8,10},{9,11},{10,... | collective-permute-start | bytes 417800 | tf_op jit(solution)/shard_map/ppermute | solution.py:40
  18.3 7.4 %collective-permute-start.6 = (bf16[3,136,512]{2,1,0:T(8,128)(2,1)}, bf16[3,136,512]{2,1,0:T(8,128)(2,1)S(1)}, u32[]{:S(2)}, u32[]{:S(2)}) collective-permute-start(bf16[3,136,512]{2,1,0:T(8,128)(2,1)} %pad_maximum_fusion), channel_id=1, source_target_pairs={{0,1},{1,0},{2,3},{3,2},{4,5},{5,4},{6,7},{7,6},{8,9},{9,8},{10,11... | collective-permute-start | bytes 1253384 | tf_op jit(solution)/shard_map/ppermute | solution.py:40
  25.7 8.4 %collective-permute-start.7 = (bf16[3,136,512]{2,1,0:T(8,128)(2,1)}, bf16[3,136,512]{2,1,0:T(8,128)(2,1)S(1)}, u32[]{:S(2)}, u32[]{:S(2)}) collective-permute-start(bf16[3,136,512]{2,1,0:T(8,128)(2,1)} %pad_maximum_fusion), channel_id=1, source_target_pairs={{0,2},{1,3},{2,0},{3,1},{4,6},{5,7},{6,4},{7,5},{8,10},{9,11},{10,... | collective-permute-start | bytes 1253384 | tf_op jit(solution)/shard_map/ppermute | solution.py:40
  27.0 10.5 %collective-permute-start.8 = (bf16[3,136,512]{2,1,0:T(8,128)(2,1)S(1)}, bf16[3,136,512]{2,1,0:T(8,128)(2,1)S(1)}, u32[]{:S(2)}, u32[]{:S(2)}) collective-permute-start(bf16[3,136,512]{2,1,0:T(8,128)(2,1)S(1)} %collective-permute-done.6.refs_2_), channel_id=1, source_target_pairs={{0,2},{1,3},{2,0},{3,1},{4,6},{5,7},{6,4},{7,5},{8,10},{9,11},{10,... | collective-permute-start | bytes 1253384 | tf_op jit(solution)/shard_map/ppermute | solution.py:40
  32.5 24.4 %collective-permute-start.19 = (bf16[8,136,512]{2,1,0:T(8,128)(2,1)}, bf16[8,136,512]{2,1,0:T(8,128)(2,1)}, u32[]{:S(2)}, u32[]{:S(2)}) collective-permute-start(bf16[8,136,512]{2,1,0:T(8,128)(2,1)} %get-tuple-element.77), channel_id=1, source_target_pairs={{0,2},{1,3},{2,0},{3,1},{4,6},{5,7},{6,4},{7,5},{8,10},{9,11},{10,... | collective-permute-start | bytes 3342344 | tf_op jit(solution)/shard_map/ppermute | solution.py:40
  42.4 6.7 %collective-permute-start.9 = (bf16[136,1536]{1,0:T(8,128)(2,1)S(1)}, bf16[136,1536]{1,0:T(8,128)(2,1)S(1)}, u32[]{:S(2)}, u32[]{:S(2)}) collective-permute-start(bf16[136,1536]{1,0:T(8,128)(2,1)S(1)} %project_2.1.refs_1_), channel_id=1, source_target_pairs={{0,16},{1,17},{2,18},{3,19},{4,20},{5,21},{6,22},{7,23},{8,24},{9,... | collective-permute-start | bytes 1253384 | tf_op jit(solution)/shard_map/ppermute | solution.py:483
  51.4 4.4 %collective-permute-start.13 = (bf16[136,512]{1,0:T(8,128)(2,1)S(1)}, bf16[136,512]{1,0:T(8,128)(2,1)S(1)}, u32[]{:S(2)}, u32[]{:S(2)}) collective-permute-start(bf16[136,512]{1,0:T(8,128)(2,1)S(1)} %get-tuple-element.67.refs_0_), channel_id=1, source_target_pairs={{0,1},{1,0},{2,3},{3,2},{4,5},{5,4},{6,7},{7,6},{8,9},{9,8},{10,11... | collective-permute-start | bytes 417800 | tf_op jit(solution)/shard_map/ppermute | solution.py:40
  53.0 11.7 %collective-permute-start.12 = (bf16[136,512]{1,0:T(8,128)(2,1)S(1)}, bf16[136,512]{1,0:T(8,128)(2,1)S(1)}, u32[]{:S(2)}, u32[]{:S(2)}) collective-permute-start(bf16[136,512]{1,0:T(8,128)(2,1)S(1)} %get-tuple-element.67.refs_0_), channel_id=1, source_target_pairs={{0,12},{1,13},{2,14},{3,15},{4,0},{5,1},{6,2},{7,3},{8,4},{9,5},{1... | collective-permute-start | bytes 417800 | tf_op jit(solution)/shard_map/ppermute | solution.py:45
  53.0 11.7 %collective-permute-start.11 = (bf16[136,512]{1,0:T(8,128)(2,1)S(1)}, bf16[136,512]{1,0:T(8,128)(2,1)S(1)}, u32[]{:S(2)}, u32[]{:S(2)}) collective-permute-start(bf16[136,512]{1,0:T(8,128)(2,1)S(1)} %get-tuple-element.67.refs_0_), channel_id=1, source_target_pairs={{0,8},{1,9},{2,10},{3,11},{4,12},{5,13},{6,14},{7,15},{8,0},{9,1},... | collective-permute-start | bytes 417800 | tf_op jit(solution)/shard_map/ppermute | solution.py:45
  53.7 11.6 %collective-permute-start.10 = (bf16[136,512]{1,0:T(8,128)(2,1)S(1)}, bf16[136,512]{1,0:T(8,128)(2,1)S(1)}, u32[]{:S(2)}, u32[]{:S(2)}) collective-permute-start(bf16[136,512]{1,0:T(8,128)(2,1)S(1)} %get-tuple-element.67.refs_0_), channel_id=1, source_target_pairs={{0,4},{1,5},{2,6},{3,7},{4,8},{5,9},{6,10},{7,11},{8,12},{9,13},{1... | collective-permute-start | bytes 417800 | tf_op jit(solution)/shard_map/ppermute | solution.py:45
  55.8 9.5 %collective-permute-start.14 = (bf16[136,512]{1,0:T(8,128)(2,1)S(1)}, bf16[136,512]{1,0:T(8,128)(2,1)S(1)}, u32[]{:S(2)}, u32[]{:S(2)}) collective-permute-start(bf16[136,512]{1,0:T(8,128)(2,1)S(1)} %get-tuple-element.67.refs_0_), channel_id=1, source_target_pairs={{0,2},{1,3},{2,0},{3,1},{4,6},{5,7},{6,4},{7,5},{8,10},{9,11},{10,... | collective-permute-start | bytes 417800 | tf_op jit(solution)/shard_map/ppermute | solution.py:40
  56.9 8.4 %collective-permute-start.15 = (bf16[136,512]{1,0:T(8,128)(2,1)S(1)}, bf16[136,512]{1,0:T(8,128)(2,1)S(1)}, u32[]{:S(2)}, u32[]{:S(2)}) collective-permute-start(bf16[136,512]{1,0:T(8,128)(2,1)S(1)} %collective-permute-done.13.refs_1_), channel_id=1, source_target_pairs={{0,2},{1,3},{2,0},{3,1},{4,6},{5,7},{6,4},{7,5},{8,10},{9,11},{10,... | collective-permute-start | bytes 417800 | tf_op jit(solution)/shard_map/ppermute | solution.py:40
  64.6 14.6 %collective-permute-start.20 = (bf16[4,136,512]{2,1,0:T(8,128)(2,1)S(1)}, bf16[4,136,512]{2,1,0:T(8,128)(2,1)S(1)}, u32[]{:S(2)}, u32[]{:S(2)}) collective-permute-start(bf16[4,136,512]{2,1,0:T(8,128)(2,1)S(1)} %add_convert_fusion.1), channel_id=1, source_target_pairs={{0,1},{1,0},{2,3},{3,2},{4,5},{5,4},{6,7},{7,6},{8,9},{9,8},{10,11... | collective-permute-start | bytes 1671176 | tf_op jit(solution)/shard_map/ppermute | solution.py:40
  65.3 12.4 %collective-permute-start.16 = (bf16[3,136,512]{2,1,0:T(8,128)(2,1)S(1)}, bf16[3,136,512]{2,1,0:T(8,128)(2,1)S(1)}, u32[]{:S(2)}, u32[]{:S(2)}) collective-permute-start(bf16[3,136,512]{2,1,0:T(8,128)(2,1)S(1)} %pad_maximum_fusion.1), channel_id=1, source_target_pairs={{0,1},{1,0},{2,3},{3,2},{4,5},{5,4},{6,7},{7,6},{8,9},{9,8},{10,11... | collective-permute-start | bytes 1253384 | tf_op jit(solution)/shard_map/ppermute | solution.py:40
  77.8 8.2 %collective-permute-start.17 = (bf16[3,136,512]{2,1,0:T(8,128)(2,1)S(1)}, bf16[3,136,512]{2,1,0:T(8,128)(2,1)S(1)}, u32[]{:S(2)}, u32[]{:S(2)}) collective-permute-start(bf16[3,136,512]{2,1,0:T(8,128)(2,1)S(1)} %pad_maximum_fusion.1), channel_id=1, source_target_pairs={{0,2},{1,3},{2,0},{3,1},{4,6},{5,7},{6,4},{7,5},{8,10},{9,11},{10,... | collective-permute-start | bytes 1253384 | tf_op jit(solution)/shard_map/ppermute | solution.py:40
  77.8 11.7 %collective-permute-start.18 = (bf16[3,136,512]{2,1,0:T(8,128)(2,1)S(1)}, bf16[3,136,512]{2,1,0:T(8,128)(2,1)S(1)}, u32[]{:S(2)}, u32[]{:S(2)}) collective-permute-start(bf16[3,136,512]{2,1,0:T(8,128)(2,1)S(1)} %collective-permute-done.16.refs_2_), channel_id=1, source_target_pairs={{0,2},{1,3},{2,0},{3,1},{4,6},{5,7},{6,4},{7,5},{8,10},{9,11},{10,... | collective-permute-start | bytes 1253384 | tf_op jit(solution)/shard_map/ppermute | solution.py:40
  80.6 10.8 %collective-permute-start.21 = (bf16[136,512]{1,0:T(8,128)(2,1)S(1)}, bf16[136,512]{1,0:T(8,128)(2,1)S(1)}, u32[]{:S(2)}, u32[]{:S(2)}) collective-permute-start(bf16[136,512]{1,0:T(8,128)(2,1)S(1)} %get-tuple-element.82), channel_id=1, source_target_pairs={{0,4},{1,5},{2,6},{3,7},{4,8},{5,9},{6,10},{7,11},{8,12},{9,13},{1... | collective-permute-start | bytes 417800 | tf_op jit(solution)/shard_map/ppermute | solution.py:45
  80.6 10.7 %collective-permute-start.22 = (bf16[136,512]{1,0:T(8,128)(2,1)S(1)}, bf16[136,512]{1,0:T(8,128)(2,1)S(1)}, u32[]{:S(2)}, u32[]{:S(2)}) collective-permute-start(bf16[136,512]{1,0:T(8,128)(2,1)S(1)} %get-tuple-element.83), channel_id=1, source_target_pairs={{0,8},{1,9},{2,10},{3,11},{4,12},{5,13},{6,14},{7,15},{8,0},{9,1},... | collective-permute-start | bytes 417800 | tf_op jit(solution)/shard_map/ppermute | solution.py:45
  80.7 13.8 %collective-permute-start.23 = (bf16[136,512]{1,0:T(8,128)(2,1)S(1)}, bf16[136,512]{1,0:T(8,128)(2,1)S(1)}, u32[]{:S(2)}, u32[]{:S(2)}) collective-permute-start(bf16[136,512]{1,0:T(8,128)(2,1)S(1)} %get-tuple-element.84), channel_id=1, source_target_pairs={{0,12},{1,13},{2,14},{3,15},{4,0},{5,1},{6,2},{7,3},{8,4},{9,5},{1... | collective-permute-start | bytes 417800 | tf_op jit(solution)/shard_map/ppermute | solution.py:45
  (14 other events, 85.1 us)

commit v2 on v1

--- a/solution.py
+++ b/solution.py
@@ -13,7 +13,7 @@
 VMEM_SPEC = pl.BlockSpec(memory_space=pltpu.VMEM)
 SMEM_SPEC = pl.BlockSpec(memory_space=pltpu.SMEM)
 HBM_SPEC = pl.BlockSpec(memory_space=pltpu.HBM)
-WEIGHT_SLOTS = 4
+WEIGHT_SLOTS = 6
 VMEM_LIMIT = 47 * 2**20
 SMALL_LIMIT = 16 * 2**20
 

time: 99.2 us -> 98.4 us (level)
  Pallas kernels: 35.8 us -> 34.6 us
    pallas_call x6, Pallas kernels: 22.7 us -> 21.4 us  [accumulate(): pl.pallas_call(functools.partial(accumulate_kernel, counts, total is not...]
    ppermute x14, waiting for transfers between devices: 14.9 us -> 16.1 us  [swap_low(): return lax.ppermute(block, ('row', 'col'), route)]
  transfers between devices with their start and end apart: 26 -> 26, of which waited for: 9 -> 11; matrix products, arithmetic and copies ran while one was open for 3% -> 3% of each run, Pallas kernels for 34% -> 33%
where the time goes in v2:
time: 98.4 us; the launch traced here: 98 us
  Pallas kernels  34.6 us (35%)
  waiting for transfers between devices  32.2 us (33%)
  starting transfers between devices  22.8 us (23%)
  local copies, waits for them, and re-layouts  4.25 us (4%)
  other arithmetic  3.32 us (3%)
    pallas_call x6, Pallas kernels, accumulate(): pl.pallas_call(functools.partial(accumulate_kernel, counts, total is not...  21.4 us
    ppermute x14, waiting for transfers between devices, swap_low(): return lax.ppermute(block, ('row', 'col'), route)  16.1 us
    ppermute x14, starting transfers between devices, swap_low(): return lax.ppermute(block, ('row', 'col'), route)  12.2 us
    ppermute x9, waiting for transfers between devices, shift_high(): return lax.ppermute(block, 'col', route)  9.59 us
    ppermute x9, starting transfers between devices, shift_high(): return lax.ppermute(block, 'col', route)  8.75 us
    pallas_call x1, Pallas kernels, partials(): pl.pallas_call(partials_kernel, out_shape=[jax.ShapeDtypeStruct((count, r...  7.62 us
    ppermute x1, waiting for transfers between devices, local(): lax.ppermute(projected, 'row', [(r, r + 1) for r in range(row_size - 1)])  5.4 us
    unnamed x24, local copies, waits for them, and re-layouts  3.86 us
  transfers between devices with their start and end apart: 26, of which 11 were waited for; matrix products, arithmetic and copies ran while one was open for 3% of the time, Pallas kernels for 33%

profile of v2, /device:TPU:9, one launch (start us, length us, event | category | flops | bytes accessed | tf_op | source)
XLA Modules:
  0.0 98.0 jit_solution(7534873068439688039)
XLA Ops:
  2.1 2.3 %collective-permute-start.1 = (bf16[136,512]{1,0:T(8,128)(2,1)}, bf16[136,512]{1,0:T(8,128)(2,1)S(1)}, u32[]{:S(2)}, u32[]{:S(2)}) collective-permute-start(bf16[136,512]{1,0:T(8,128)(2,1)} %refs_0_.1), channel_id=1, source_target_pairs={{0,8},{1,9},{2,10},{3,11},{4,12},{5,13},{6,14},{7,15},{8,0},{9,1},... | collective-permute-start | bytes 417800 | tf_op jit(solution)/shard_map/ppermute | solution.py:45
  4.4 2.2 %collective-permute-start = (bf16[136,512]{1,0:T(8,128)(2,1)}, bf16[136,512]{1,0:T(8,128)(2,1)S(1)}, u32[]{:S(2)}, u32[]{:S(2)}) collective-permute-start(bf16[136,512]{1,0:T(8,128)(2,1)} %refs_0_.1), channel_id=1, source_target_pairs={{0,4},{1,5},{2,6},{3,7},{4,8},{5,9},{6,10},{7,11},{8,12},{9,13},{1... | collective-permute-start | bytes 417800 | tf_op jit(solution)/shard_map/ppermute | solution.py:45
  9.1 7.6 %grad_partials.1 = (bf16[4,136,512]{2,1,0:T(8,128)(2,1)S(1)}, bf16[4,136,512]{2,1,0:T(8,128)(2,1)S(1)}, bf16[8,136,512]{2,1,0:T(8,128)(2,1)}) custom-call(s32[16]{0:T(128)S(1)} %stack.156.owners, bf16[136,512]{1,0:T(8,128)(2,1)S(1)} %copy-done.1, bf16[8192,512]{1,0:T(8,128)(2,1)} %refs_4_.5), custom_call_target="tpu_custom_call" | custom-call | flops 1140850688 | bytes 10616832 | tf_op jit(solution)/shard_map/grad_partials/pallas_call | solution.py:236
  21.0 4.3 %project_0.1.refs_3_ = f32[136,1536]{1,0:T(8,128)S(1)} custom-call(s32[5]{0:T(128)S(1)} %stack.163.owners, bf16[136,512]{1,0:T(8,128)(2,1)S(1)} %copy-done.2, bf16[136,512]{1,0:T(8,128)(2,1)S(1)} %collective-permute-done.3.refs_1_, bf16[136,512]{1,0:T(8,128)(2,1)S(1)} %collective-permute-done.refs_2_, bf16[136,512]{1,0:T(8,128)(2,1)S(1)} %collective-permute-done.1.refs_3_, ...), custom_call_target="tpu_custom_call" | custom-call | flops 1069547520 | bytes 9535488 | tf_op jit(solution)/shard_map/project_0/pallas_call | solution.py:181
  25.7 1.3 %collective-permute-start.7 = (bf16[3,136,512]{2,1,0:T(8,128)(2,1)}, bf16[3,136,512]{2,1,0:T(8,128)(2,1)S(1)}, u32[]{:S(2)}, u32[]{:S(2)}) collective-permute-start(bf16[3,136,512]{2,1,0:T(8,128)(2,1)} %pad_maximum_fusion), channel_id=1, source_target_pairs={{0,2},{1,3},{2,0},{3,1},{4,6},{5,7},{6,4},{7,5},{8,10},{9,11},{10,... | collective-permute-start | bytes 1253384 | tf_op jit(solution)/shard_map/ppermute | solution.py:40
  28.1 4.3 %project_1.1.refs_2_ = f32[136,1536]{1,0:T(8,128)S(1)} custom-call(s32[11]{0:T(128)S(1)} %stack.166.owners, bf16[136,512]{1,0:T(8,128)(2,1)S(1)} %copy-done.4, bf16[136,512]{1,0:T(8,128)(2,1)S(1)} %copy-done.6, bf16[3,136,512]{2,1,0:T(8,128)(2,1)S(1)} %collective-permute-done.6.refs_2_, f32[136,1536]{1,0:T(8,128)S(1)} %project_0.1.refs_3_, ...), custom_call_target="tpu_custom_call" | custom-call | flops 1069547520 | bytes 9535488 | tf_op jit(solution)/shard_map/project_1/pallas_call | solution.py:181
  32.4 1.4 %collective-permute-start.19 = (bf16[8,136,512]{2,1,0:T(8,128)(2,1)}, bf16[8,136,512]{2,1,0:T(8,128)(2,1)}, u32[]{:S(2)}, u32[]{:S(2)}) collective-permute-start(bf16[8,136,512]{2,1,0:T(8,128)(2,1)} %get-tuple-element.77), channel_id=1, source_target_pairs={{0,2},{1,3},{2,0},{3,1},{4,6},{5,7},{6,4},{7,5},{8,10},{9,11},{10,... | collective-permute-start | bytes 3342344 | tf_op jit(solution)/shard_map/ppermute | solution.py:40
  33.9 3.7 %collective-permute-done.8.refs_1_ = bf16[3,136,512]{2,1,0:T(8,128)(2,1)S(1)} collective-permute-done((bf16[3,136,512]{2,1,0:T(8,128)(2,1)S(1)}, bf16[3,136,512]{2,1,0:T(8,128)(2,1)S(1)}, u32[]{:S(2)}, u32[]{:S(2)}) %collective-permute-start.8) | collective-permute-done | bytes 417824 | tf_op jit(solution)/shard_map/ppermute | solution.py:40
  37.6 4.7 %project_2.1.refs_1_ = bf16[136,1536]{1,0:T(8,128)(2,1)S(1)} custom-call(s32[6]{0:T(128)S(1)} %stack.70.owners, bf16[3,136,512]{2,1,0:T(8,128)(2,1)S(1)} %collective-permute-done.7.refs_0_, bf16[3,136,512]{2,1,0:T(8,128)(2,1)S(1)} %collective-permute-done.8.refs_1_, f32[136,1536]{1,0:T(8,128)S(1)} %project_1.1.refs_2_, bf16[8192,1536]{1,0:T(8,128)(2,1)} %refs_3_.1), custom_call_target="tpu_custom_call" | custom-call | flops 1283457024 | bytes 11108352 | tf_op jit(solution)/shard_map/project_2/pallas_call | solution.py:181
  43.6 5.4 %collective-permute-done.9.refs_0_ = bf16[136,1536]{1,0:T(8,128)(2,1)S(1)} collective-permute-done((bf16[136,1536]{1,0:T(8,128)(2,1)S(1)}, bf16[136,1536]{1,0:T(8,128)(2,1)S(1)}, u32[]{:S(2)}, u32[]{:S(2)}) %collective-permute-start.9) | collective-permute-done | bytes 417824 | tf_op jit(solution)/shard_map/ppermute | solution.py:483
  49.0 2.3 %mixing.1 = (bf16[136,512]{1,0:T(8,128)(2,1)S(1)}, f32[136,512]{1,0:T(8,128)S(1)}, f32[272,512]{1,0:T(8,128)S(1)}) custom-call(bf16[136,1536]{1,0:T(8,128)(2,1)S(1)} %collective-permute-done.9.refs_0_, bf16[136,1536]{1,0:T(8,128)(2,1)S(1)} %project_2.1.refs_1_, bf16[384,384]{1,0:T(8,128)(2,1)S(1)} %copy-done, f32[3,1536]{1,0:T(4,128)S(1)} %get-tuple-element.60.refs_3_, ...), custom_call_target="tpu_custom_call" | custom-call | flops 1140850688 | bytes 3489792 | tf_op jit(solution)/shard_map/mixing/pallas_call | solution.py:352
  51.3 1.7 %collective-permute-start.13 = (bf16[136,512]{1,0:T(8,128)(2,1)S(1)}, bf16[136,512]{1,0:T(8,128)(2,1)S(1)}, u32[]{:S(2)}, u32[]{:S(2)}) collective-permute-start(bf16[136,512]{1,0:T(8,128)(2,1)S(1)} %get-tuple-element.67.refs_0_), channel_id=1, source_target_pairs={{0,1},{1,0},{2,3},{3,2},{4,5},{5,4},{6,7},{7,6},{8,9},{9,8},{10,11... | collective-permute-start | bytes 417800 | tf_op jit(solution)/shard_map/ppermute | solution.py:40
  53.5 2.1 %collective-permute-start.10 = (bf16[136,512]{1,0:T(8,128)(2,1)S(1)}, bf16[136,512]{1,0:T(8,128)(2,1)S(1)}, u32[]{:S(2)}, u32[]{:S(2)}) collective-permute-start(bf16[136,512]{1,0:T(8,128)(2,1)S(1)} %get-tuple-element.67.refs_0_), channel_id=1, source_target_pairs={{0,4},{1,5},{2,6},{3,7},{4,8},{5,9},{6,10},{7,11},{8,12},{9,13},{1... | collective-permute-start | bytes 417800 | tf_op jit(solution)/shard_map/ppermute | solution.py:45
  58.4 6.2 %collective-permute-done.12.refs_4_ = bf16[136,512]{1,0:T(8,128)(2,1)S(1)} collective-permute-done((bf16[136,512]{1,0:T(8,128)(2,1)S(1)}, bf16[136,512]{1,0:T(8,128)(2,1)S(1)}, u32[]{:S(2)}, u32[]{:S(2)}) %collective-permute-start.12) | collective-permute-done | bytes 139296 | tf_op jit(solution)/shard_map/ppermute | solution.py:45
  65.3 1.5 %collective-permute-start.16 = (bf16[3,136,512]{2,1,0:T(8,128)(2,1)S(1)}, bf16[3,136,512]{2,1,0:T(8,128)(2,1)S(1)}, u32[]{:S(2)}, u32[]{:S(2)}) collective-permute-start(bf16[3,136,512]{2,1,0:T(8,128)(2,1)S(1)} %pad_maximum_fusion.1), channel_id=1, source_target_pairs={{0,1},{1,0},{2,3},{3,2},{4,5},{5,4},{6,7},{7,6},{8,9},{9,8},{10,11... | collective-permute-start | bytes 1253384 | tf_op jit(solution)/shard_map/ppermute | solution.py:40
  66.8 2.5 %output_0.1.refs_3_ = f32[136,512]{1,0:T(8,128)S(1)} custom-call(s32[5]{0:T(128)S(1)} %stack.163.owners, bf16[136,512]{1,0:T(8,128)(2,1)S(1)} %get-tuple-element.67.refs_0_, bf16[136,512]{1,0:T(8,128)(2,1)S(1)} %collective-permute-done.13.refs_1_, bf16[136,512]{1,0:T(8,128)(2,1)S(1)} %collective-permute-done.10.refs_2_, ...), custom_call_target="tpu_custom_call" | custom-call | flops 356515840 | bytes 3178496 | tf_op jit(solution)/shard_map/output_0/pallas_call | solution.py:181
  69.3 8.1 %collective-permute-done.16.refs_2_ = bf16[3,136,512]{2,1,0:T(8,128)(2,1)S(1)} collective-permute-done((bf16[3,136,512]{2,1,0:T(8,128)(2,1)S(1)}, bf16[3,136,512]{2,1,0:T(8,128)(2,1)S(1)}, u32[]{:S(2)}, u32[]{:S(2)}) %collective-permute-start.16) | collective-permute-done | bytes 417824 | tf_op jit(solution)/shard_map/ppermute | solution.py:40
  77.5 1.5 %collective-permute-start.18 = (bf16[3,136,512]{2,1,0:T(8,128)(2,1)S(1)}, bf16[3,136,512]{2,1,0:T(8,128)(2,1)S(1)}, u32[]{:S(2)}, u32[]{:S(2)}) collective-permute-start(bf16[3,136,512]{2,1,0:T(8,128)(2,1)S(1)} %collective-permute-done.16.refs_2_), channel_id=1, source_target_pairs={{0,2},{1,3},{2,0},{3,1},{4,6},{5,7},{6,4},{7,5},{8,10},{9,11},{10,... | collective-permute-start | bytes 1253384 | tf_op jit(solution)/shard_map/ppermute | solution.py:40
  80.4 1.4 %collective-permute-start.23 = (bf16[136,512]{1,0:T(8,128)(2,1)S(1)}, bf16[136,512]{1,0:T(8,128)(2,1)S(1)}, u32[]{:S(2)}, u32[]{:S(2)}) collective-permute-start(bf16[136,512]{1,0:T(8,128)(2,1)S(1)} %get-tuple-element.84), channel_id=1, source_target_pairs={{0,12},{1,13},{2,14},{3,15},{4,0},{5,1},{6,2},{7,3},{8,4},{9,5},{1... | collective-permute-start | bytes 417800 | tf_op jit(solution)/shard_map/ppermute | solution.py:45
  81.8 3.7 %output_1.1 = (f32[136,512]{1,0:T(8,128)S(1)}, bf16[6,512,512]{2,1,0:T(8,128)(2,1)S(1)}) custom-call(s32[11]{0:T(128)S(1)} %stack.166.owners, bf16[136,512]{1,0:T(8,128)(2,1)S(1)} %collective-permute-done.14.refs_0_, bf16[136,512]{1,0:T(8,128)(2,1)S(1)} %collective-permute-done.15.refs_1_, bf16[3,136,512]{2,1,0:T(8,128)(2,1)S(1)} %collective-permute-done.16.refs_2_, ...), custom_call_target="tpu_custom_call" | custom-call | flops 356515840 | bytes 6324224 | tf_op jit(solution)/shard_map/output_1/pallas_call | solution.py:181
  85.5 3.7 %collective-permute-done.18.refs_1_ = bf16[3,136,512]{2,1,0:T(8,128)(2,1)S(1)} collective-permute-done((bf16[3,136,512]{2,1,0:T(8,128)(2,1)S(1)}, bf16[3,136,512]{2,1,0:T(8,128)(2,1)S(1)}, u32[]{:S(2)}, u32[]{:S(2)}) %collective-permute-start.18) | collective-permute-done | bytes 417824 | tf_op jit(solution)/shard_map/ppermute | solution.py:40
  89.1 1.9 %output_2.1 = bf16[136,512]{1,0:T(8,128)(2,1)} custom-call(s32[6]{0:T(128)S(1)} %stack.70.owners, bf16[3,136,512]{2,1,0:T(8,128)(2,1)S(1)} %collective-permute-done.17.refs_0_, bf16[3,136,512]{2,1,0:T(8,128)(2,1)S(1)} %collective-permute-done.18.refs_1_, f32[136,512]{1,0:T(8,128)S(1)} %get-tuple-element.74.refs_2_, ...), custom_call_target="tpu_custom_call" | custom-call | flops 427819008 | bytes 3702784 | tf_op jit(solution)/shard_map/output_2/pallas_call | solution.py:181
  91.3 2.6 %collective-permute-done.23.refs_3_ = bf16[136,512]{1,0:T(8,128)(2,1)S(1)} collective-permute-done((bf16[136,512]{1,0:T(8,128)(2,1)S(1)}, bf16[136,512]{1,0:T(8,128)(2,1)S(1)}, u32[]{:S(2)}, u32[]{:S(2)}) %collective-permute-start.23) | collective-permute-done | bytes 139296 | tf_op jit(solution)/shard_map/ppermute | solution.py:45
  93.8 1.9 %tap_grad.1 = (f32[32,128]{1,0:T(8,128)S(1)}, f32[1,512]{1,0:T(1,128)S(1)}) custom-call(bf16[136,512]{1,0:T(8,128)(2,1)S(1)} %get-tuple-element.85.refs_0_, bf16[136,512]{1,0:T(8,128)(2,1)S(1)} %collective-permute-done.21.refs_1_, bf16[136,512]{1,0:T(8,128)(2,1)S(1)} %collective-permute-done.22.refs_2_, ...), custom_call_target="tpu_custom_call" | custom-call | flops 570425344 | bytes 974848 | tf_op jit(solution)/shard_map/tap_grad/pallas_call | solution.py:426
  (72 shorter events, 18.9 us)
Async XLA Ops:
  0.6 6.0 %collective-permute-start.3 = (bf16[136,512]{1,0:T(8,128)(2,1)}, bf16[136,512]{1,0:T(8,128)(2,1)S(1)}, u32[]{:S(2)}, u32[]{:S(2)}) collective-permute-start(bf16[136,512]{1,0:T(8,128)(2,1)} %refs_0_.1), channel_id=1, source_target_pairs={{0,1},{1,0},{2,3},{3,2},{4,5},{5,4},{6,7},{7,6},{8,9},{9,8},{10,11... | collective-permute-start | bytes 417800 | tf_op jit(solution)/shard_map/ppermute | solution.py:40
  1.9 14.8 %collective-permute-start.2 = (bf16[136,512]{1,0:T(8,128)(2,1)}, bf16[136,512]{1,0:T(8,128)(2,1)S(1)}, u32[]{:S(2)}, u32[]{:S(2)}) collective-permute-start(bf16[136,512]{1,0:T(8,128)(2,1)} %refs_0_.1), channel_id=1, source_target_pairs={{0,12},{1,13},{2,14},{3,15},{4,0},{5,1},{6,2},{7,3},{8,4},{9,5},{1... | collective-permute-start | bytes 417800 | tf_op jit(solution)/shard_map/ppermute | solution.py:45
  2.1 14.6 %collective-permute-start.1 = (bf16[136,512]{1,0:T(8,128)(2,1)}, bf16[136,512]{1,0:T(8,128)(2,1)S(1)}, u32[]{:S(2)}, u32[]{:S(2)}) collective-permute-start(bf16[136,512]{1,0:T(8,128)(2,1)} %refs_0_.1), channel_id=1, source_target_pairs={{0,8},{1,9},{2,10},{3,11},{4,12},{5,13},{6,14},{7,15},{8,0},{9,1},... | collective-permute-start | bytes 417800 | tf_op jit(solution)/shard_map/ppermute | solution.py:45
  4.4 12.3 %collective-permute-start = (bf16[136,512]{1,0:T(8,128)(2,1)}, bf16[136,512]{1,0:T(8,128)(2,1)S(1)}, u32[]{:S(2)}, u32[]{:S(2)}) collective-permute-start(bf16[136,512]{1,0:T(8,128)(2,1)} %refs_0_.1), channel_id=1, source_target_pairs={{0,4},{1,5},{2,6},{3,7},{4,8},{5,9},{6,10},{7,11},{8,12},{9,13},{1... | collective-permute-start | bytes 417800 | tf_op jit(solution)/shard_map/ppermute | solution.py:45
  6.6 10.2 %collective-permute-start.4 = (bf16[136,512]{1,0:T(8,128)(2,1)}, bf16[136,512]{1,0:T(8,128)(2,1)S(1)}, u32[]{:S(2)}, u32[]{:S(2)}) collective-permute-start(bf16[136,512]{1,0:T(8,128)(2,1)} %refs_0_.1), channel_id=1, source_target_pairs={{0,2},{1,3},{2,0},{3,1},{4,6},{5,7},{6,4},{7,5},{8,10},{9,11},{10,... | collective-permute-start | bytes 417800 | tf_op jit(solution)/shard_map/ppermute | solution.py:40
  7.8 9.0 %collective-permute-start.5 = (bf16[136,512]{1,0:T(8,128)(2,1)S(1)}, bf16[136,512]{1,0:T(8,128)(2,1)S(1)}, u32[]{:S(2)}, u32[]{:S(2)}) collective-permute-start(bf16[136,512]{1,0:T(8,128)(2,1)S(1)} %collective-permute-done.3.refs_1_), channel_id=1, source_target_pairs={{0,2},{1,3},{2,0},{3,1},{4,6},{5,7},{6,4},{7,5},{8,10},{9,11},{10,... | collective-permute-start | bytes 417800 | tf_op jit(solution)/shard_map/ppermute | solution.py:40
  18.3 7.4 %collective-permute-start.6 = (bf16[3,136,512]{2,1,0:T(8,128)(2,1)}, bf16[3,136,512]{2,1,0:T(8,128)(2,1)S(1)}, u32[]{:S(2)}, u32[]{:S(2)}) collective-permute-start(bf16[3,136,512]{2,1,0:T(8,128)(2,1)} %pad_maximum_fusion), channel_id=1, source_target_pairs={{0,1},{1,0},{2,3},{3,2},{4,5},{5,4},{6,7},{7,6},{8,9},{9,8},{10,11... | collective-permute-start | bytes 1253384 | tf_op jit(solution)/shard_map/ppermute | solution.py:40
  25.7 8.2 %collective-permute-start.7 = (bf16[3,136,512]{2,1,0:T(8,128)(2,1)}, bf16[3,136,512]{2,1,0:T(8,128)(2,1)S(1)}, u32[]{:S(2)}, u32[]{:S(2)}) collective-permute-start(bf16[3,136,512]{2,1,0:T(8,128)(2,1)} %pad_maximum_fusion), channel_id=1, source_target_pairs={{0,2},{1,3},{2,0},{3,1},{4,6},{5,7},{6,4},{7,5},{8,10},{9,11},{10,... | collective-permute-start | bytes 1253384 | tf_op jit(solution)/shard_map/ppermute | solution.py:40
  27.0 10.5 %collective-permute-start.8 = (bf16[3,136,512]{2,1,0:T(8,128)(2,1)S(1)}, bf16[3,136,512]{2,1,0:T(8,128)(2,1)S(1)}, u32[]{:S(2)}, u32[]{:S(2)}) collective-permute-start(bf16[3,136,512]{2,1,0:T(8,128)(2,1)S(1)} %collective-permute-done.6.refs_2_), channel_id=1, source_target_pairs={{0,2},{1,3},{2,0},{3,1},{4,6},{5,7},{6,4},{7,5},{8,10},{9,11},{10,... | collective-permute-start | bytes 1253384 | tf_op jit(solution)/shard_map/ppermute | solution.py:40
  32.4 24.4 %collective-permute-start.19 = (bf16[8,136,512]{2,1,0:T(8,128)(2,1)}, bf16[8,136,512]{2,1,0:T(8,128)(2,1)}, u32[]{:S(2)}, u32[]{:S(2)}) collective-permute-start(bf16[8,136,512]{2,1,0:T(8,128)(2,1)} %get-tuple-element.77), channel_id=1, source_target_pairs={{0,2},{1,3},{2,0},{3,1},{4,6},{5,7},{6,4},{7,5},{8,10},{9,11},{10,... | collective-permute-start | bytes 3342344 | tf_op jit(solution)/shard_map/ppermute | solution.py:40
  42.3 6.7 %collective-permute-start.9 = (bf16[136,1536]{1,0:T(8,128)(2,1)S(1)}, bf16[136,1536]{1,0:T(8,128)(2,1)S(1)}, u32[]{:S(2)}, u32[]{:S(2)}) collective-permute-start(bf16[136,1536]{1,0:T(8,128)(2,1)S(1)} %project_2.1.refs_1_), channel_id=1, source_target_pairs={{0,16},{1,17},{2,18},{3,19},{4,20},{5,21},{6,22},{7,23},{8,24},{9,... | collective-permute-start | bytes 1253384 | tf_op jit(solution)/shard_map/ppermute | solution.py:483
  51.3 4.5 %collective-permute-start.13 = (bf16[136,512]{1,0:T(8,128)(2,1)S(1)}, bf16[136,512]{1,0:T(8,128)(2,1)S(1)}, u32[]{:S(2)}, u32[]{:S(2)}) collective-permute-start(bf16[136,512]{1,0:T(8,128)(2,1)S(1)} %get-tuple-element.67.refs_0_), channel_id=1, source_target_pairs={{0,1},{1,0},{2,3},{3,2},{4,5},{5,4},{6,7},{7,6},{8,9},{9,8},{10,11... | collective-permute-start | bytes 417800 | tf_op jit(solution)/shard_map/ppermute | solution.py:40
  53.0 11.6 %collective-permute-start.12 = (bf16[136,512]{1,0:T(8,128)(2,1)S(1)}, bf16[136,512]{1,0:T(8,128)(2,1)S(1)}, u32[]{:S(2)}, u32[]{:S(2)}) collective-permute-start(bf16[136,512]{1,0:T(8,128)(2,1)S(1)} %get-tuple-element.67.refs_0_), channel_id=1, source_target_pairs={{0,12},{1,13},{2,14},{3,15},{4,0},{5,1},{6,2},{7,3},{8,4},{9,5},{1... | collective-permute-start | bytes 417800 | tf_op jit(solution)/shard_map/ppermute | solution.py:45
  53.0 11.6 %collective-permute-start.11 = (bf16[136,512]{1,0:T(8,128)(2,1)S(1)}, bf16[136,512]{1,0:T(8,128)(2,1)S(1)}, u32[]{:S(2)}, u32[]{:S(2)}) collective-permute-start(bf16[136,512]{1,0:T(8,128)(2,1)S(1)} %get-tuple-element.67.refs_0_), channel_id=1, source_target_pairs={{0,8},{1,9},{2,10},{3,11},{4,12},{5,13},{6,14},{7,15},{8,0},{9,1},... | collective-permute-start | bytes 417800 | tf_op jit(solution)/shard_map/ppermute | solution.py:45
  53.5 11.7 %collective-permute-start.10 = (bf16[136,512]{1,0:T(8,128)(2,1)S(1)}, bf16[136,512]{1,0:T(8,128)(2,1)S(1)}, u32[]{:S(2)}, u32[]{:S(2)}) collective-permute-start(bf16[136,512]{1,0:T(8,128)(2,1)S(1)} %get-tuple-element.67.refs_0_), channel_id=1, source_target_pairs={{0,4},{1,5},{2,6},{3,7},{4,8},{5,9},{6,10},{7,11},{8,12},{9,13},{1... | collective-permute-start | bytes 417800 | tf_op jit(solution)/shard_map/ppermute | solution.py:45
  55.8 9.5 %collective-permute-start.14 = (bf16[136,512]{1,0:T(8,128)(2,1)S(1)}, bf16[136,512]{1,0:T(8,128)(2,1)S(1)}, u32[]{:S(2)}, u32[]{:S(2)}) collective-permute-start(bf16[136,512]{1,0:T(8,128)(2,1)S(1)} %get-tuple-element.67.refs_0_), channel_id=1, source_target_pairs={{0,2},{1,3},{2,0},{3,1},{4,6},{5,7},{6,4},{7,5},{8,10},{9,11},{10,... | collective-permute-start | bytes 417800 | tf_op jit(solution)/shard_map/ppermute | solution.py:40
  56.8 8.5 %collective-permute-start.15 = (bf16[136,512]{1,0:T(8,128)(2,1)S(1)}, bf16[136,512]{1,0:T(8,128)(2,1)S(1)}, u32[]{:S(2)}, u32[]{:S(2)}) collective-permute-start(bf16[136,512]{1,0:T(8,128)(2,1)S(1)} %collective-permute-done.13.refs_1_), channel_id=1, source_target_pairs={{0,2},{1,3},{2,0},{3,1},{4,6},{5,7},{6,4},{7,5},{8,10},{9,11},{10,... | collective-permute-start | bytes 417800 | tf_op jit(solution)/shard_map/ppermute | solution.py:40
  64.6 14.3 %collective-permute-start.20 = (bf16[4,136,512]{2,1,0:T(8,128)(2,1)S(1)}, bf16[4,136,512]{2,1,0:T(8,128)(2,1)S(1)}, u32[]{:S(2)}, u32[]{:S(2)}) collective-permute-start(bf16[4,136,512]{2,1,0:T(8,128)(2,1)S(1)} %add_convert_fusion.1), channel_id=1, source_target_pairs={{0,1},{1,0},{2,3},{3,2},{4,5},{5,4},{6,7},{7,6},{8,9},{9,8},{10,11... | collective-permute-start | bytes 1671176 | tf_op jit(solution)/shard_map/ppermute | solution.py:40
  65.3 12.2 %collective-permute-start.16 = (bf16[3,136,512]{2,1,0:T(8,128)(2,1)S(1)}, bf16[3,136,512]{2,1,0:T(8,128)(2,1)S(1)}, u32[]{:S(2)}, u32[]{:S(2)}) collective-permute-start(bf16[3,136,512]{2,1,0:T(8,128)(2,1)S(1)} %pad_maximum_fusion.1), channel_id=1, source_target_pairs={{0,1},{1,0},{2,3},{3,2},{4,5},{5,4},{6,7},{7,6},{8,9},{9,8},{10,11... | collective-permute-start | bytes 1253384 | tf_op jit(solution)/shard_map/ppermute | solution.py:40
  77.5 8.0 %collective-permute-start.17 = (bf16[3,136,512]{2,1,0:T(8,128)(2,1)S(1)}, bf16[3,136,512]{2,1,0:T(8,128)(2,1)S(1)}, u32[]{:S(2)}, u32[]{:S(2)}) collective-permute-start(bf16[3,136,512]{2,1,0:T(8,128)(2,1)S(1)} %pad_maximum_fusion.1), channel_id=1, source_target_pairs={{0,2},{1,3},{2,0},{3,1},{4,6},{5,7},{6,4},{7,5},{8,10},{9,11},{10,... | collective-permute-start | bytes 1253384 | tf_op jit(solution)/shard_map/ppermute | solution.py:40
  77.5 11.7 %collective-permute-start.18 = (bf16[3,136,512]{2,1,0:T(8,128)(2,1)S(1)}, bf16[3,136,512]{2,1,0:T(8,128)(2,1)S(1)}, u32[]{:S(2)}, u32[]{:S(2)}) collective-permute-start(bf16[3,136,512]{2,1,0:T(8,128)(2,1)S(1)} %collective-permute-done.16.refs_2_), channel_id=1, source_target_pairs={{0,2},{1,3},{2,0},{3,1},{4,6},{5,7},{6,4},{7,5},{8,10},{9,11},{10,... | collective-permute-start | bytes 1253384 | tf_op jit(solution)/shard_map/ppermute | solution.py:40
  80.3 10.8 %collective-permute-start.21 = (bf16[136,512]{1,0:T(8,128)(2,1)S(1)}, bf16[136,512]{1,0:T(8,128)(2,1)S(1)}, u32[]{:S(2)}, u32[]{:S(2)}) collective-permute-start(bf16[136,512]{1,0:T(8,128)(2,1)S(1)} %get-tuple-element.82), channel_id=1, source_target_pairs={{0,4},{1,5},{2,6},{3,7},{4,8},{5,9},{6,10},{7,11},{8,12},{9,13},{1... | collective-permute-start | bytes 417800 | tf_op jit(solution)/shard_map/ppermute | solution.py:45
  80.3 11.0 %collective-permute-start.22 = (bf16[136,512]{1,0:T(8,128)(2,1)S(1)}, bf16[136,512]{1,0:T(8,128)(2,1)S(1)}, u32[]{:S(2)}, u32[]{:S(2)}) collective-permute-start(bf16[136,512]{1,0:T(8,128)(2,1)S(1)} %get-tuple-element.83), channel_id=1, source_target_pairs={{0,8},{1,9},{2,10},{3,11},{4,12},{5,13},{6,14},{7,15},{8,0},{9,1},... | collective-permute-start | bytes 417800 | tf_op jit(solution)/shard_map/ppermute | solution.py:45
  80.4 13.4 %collective-permute-start.23 = (bf16[136,512]{1,0:T(8,128)(2,1)S(1)}, bf16[136,512]{1,0:T(8,128)(2,1)S(1)}, u32[]{:S(2)}, u32[]{:S(2)}) collective-permute-start(bf16[136,512]{1,0:T(8,128)(2,1)S(1)} %get-tuple-element.84), channel_id=1, source_target_pairs={{0,12},{1,13},{2,14},{3,15},{4,0},{5,1},{6,2},{7,3},{8,4},{9,5},{1... | collective-permute-start | bytes 417800 | tf_op jit(solution)/shard_map/ppermute | solution.py:45
  (14 other events, 85.1 us)
